TPU v7x, 32 devices: a whole 2x2x4 slice. The times are simulated.
32 devices in a mesh: fsdp: 4 (over x, core), ctx: 8 (over z, y).
Axes of the slice: x: 2, y: 2, z: 4, core: 2. Of those that a mesh axis runs over, the one named last changes fastest.
Arguments:
- queries: bfloat16 [4, 1024, 2048], P('fsdp', 'ctx'), may hold values from -200 to 200
- keyvals: bfloat16 [4, 1024, 2, 512], P('fsdp', 'ctx'), may hold values from -6 to 6
- span_ids: int32 [4, 16], P('fsdp'), may hold values from 0 to 15, as said below
Outputs:
- attended: bfloat16 [4, 1024, 2048], P('fsdp', 'ctx')
Inputs may be any that keep to these rules, and one draw needn't show every extreme that they name: `span_ids`: in each sequence, ctx device d holds storage spans 2d and 2d+1; storage span 2d has position span p with p < 8 and storage span 2d+1 has position span 16 - 1-p; each p belongs to exactly one device.
All inputs are finite; a program needn't handle non-finite values.
Results may differ from a plain program's by a relative error of at most 0.0041.
Values may be sent and summed in bfloat16 or wider, within the bound.
No kernel may reach another device: no remote copies, remote signals or barrier semaphores. Data moves between devices by JAX's collectives and lax.ppermute only.
A program may use at most 64 MiB of HBM per device.

v0:
```python
import math

import jax
import jax.numpy as jnp
from jax import lax
from jax.sharding import PartitionSpec as P

KV_HEADS = 4
GROUP = 4
HEAD_DIM = 128


def attend_slot(state, slot_rows, slot_pos, buffer, base):
    buffer_rows = buffer.shape[0]
    key_heads = slot_rows.shape[0]
    head_width = slot_rows.shape[2]
    block_width = math.gcd(buffer_rows, 512)
    total_blocks = buffer_rows // block_width
    scale = 1.0 / math.sqrt(head_width)
    needed = (jnp.max(slot_pos) + 1 - base + block_width - 1) // block_width
    block_total = jnp.clip(needed, 0, total_blocks)
    inside = jnp.arange(block_width, dtype=jnp.int32)

    def visit(block, carry):
        running_max, running_sum, weighted = carry
        rows = lax.dynamic_slice_in_dim(buffer, block * block_width, block_width, 0)
        key_block = rows[:, 0].reshape(block_width, key_heads, head_width)
        value_block = rows[:, 1].reshape(block_width, key_heads, head_width)
        key_pos = base + block * block_width + inside
        scores = (
            jnp.einsum("hrd,nhd->hrn", slot_rows, key_block, preferred_element_type=jnp.float32)
            * scale
        )
        allowed = key_pos[None, None, :] <= slot_pos[None, :, None]
        scores = jnp.where(allowed, scores, -1e30)
        new_max = jnp.maximum(running_max, jnp.max(scores, axis=-1))
        shrink = jnp.exp(running_max - new_max)
        weights = jnp.where(allowed, jnp.exp(scores - new_max[..., None]), 0.0)
        running_sum = running_sum * shrink + jnp.sum(weights, axis=-1)
        update = jnp.einsum(
            "hrn,nhd->hrd",
            weights.astype(jnp.bfloat16),
            value_block,
            preferred_element_type=jnp.float32,
        )
        weighted = weighted * shrink[..., None] + update
        return (new_max, running_sum, weighted)

    return lax.fori_loop(0, block_total, visit, state)


def per_device(queries, keyvals, span_ids):
    tok_rows = queries.shape[1]
    span_rows = tok_rows // 2
    ctx_count = lax.axis_size("ctx")
    seq_rows = tok_rows * ctx_count
    key_heads = KV_HEADS
    group_size = GROUP
    head_width = HEAD_DIM
    feature_width = key_heads * head_width
    span_table = span_ids[0]
    device_index = lax.axis_index("ctx")
    own_spans = lax.dynamic_slice_in_dim(span_table, 2 * device_index, 2)
    offsets = jnp.arange(span_rows, dtype=jnp.int32)
    query_pos = (
        own_spans[:, None, None] * span_rows
        + jnp.zeros((1, group_size, 1), jnp.int32)
        + offsets[None, None, :]
    ).reshape(2, group_size * span_rows)
    query_rows = queries[0].reshape(2, span_rows, key_heads, group_size, head_width)
    query_rows = jnp.transpose(query_rows, (2, 0, 3, 1, 4)).reshape(
        key_heads, 2, group_size * span_rows, head_width
    )
    slot_count = group_size * span_rows

    def fresh_state():
        return (
            jnp.full((key_heads, slot_count), -1e30, jnp.float32),
            jnp.zeros((key_heads, slot_count), jnp.float32),
            jnp.zeros((key_heads, slot_count, head_width), jnp.float32),
        )

    empty = jnp.zeros((seq_rows, 2, feature_width), jnp.bfloat16)
    piece_rows = lax.all_gather(keyvals, "ctx", axis=1, tiled=True)[0]
    span_total = piece_rows.shape[0] // span_rows

    def place_one(index, current):
        position_span = lax.dynamic_index_in_dim(span_table, index, 0, False)
        rows = lax.dynamic_slice_in_dim(piece_rows, index * span_rows, span_rows, 0)
        return lax.dynamic_update_slice_in_dim(current, rows, position_span * span_rows, 0)

    buffer = lax.fori_loop(0, span_total, place_one, empty)
    first_state = attend_slot(fresh_state(), query_rows[:, 0], query_pos[0], buffer, 0)
    second_state = attend_slot(fresh_state(), query_rows[:, 1], query_pos[1], buffer, 0)
    finished = []
    for state in (first_state, second_state):
        running_max, running_sum, weighted = state
        finished.append(weighted / running_sum[..., None])
    result = jnp.stack(finished, axis=1)
    result = result.reshape(key_heads, 2, group_size, span_rows, head_width)
    attended = (
        jnp.transpose(result, (1, 3, 0, 2, 4))
        .reshape(1, tok_rows, key_heads * group_size * head_width)
        .astype(jnp.bfloat16)
    )
    return attended


def solution(mesh):
    in_specs = (P("fsdp", "ctx", None), P("fsdp", "ctx", None, None), P("fsdp", None))
    out_specs = P("fsdp", "ctx", None)
    return jax.shard_map(
        per_device, mesh=mesh, in_specs=in_specs, out_specs=out_specs, check_vma=False
    )
```

profile of v0, /device:TPU:0, one launch (start us, length us, event | category | flops | bytes accessed | tf_op | source)
XLA Modules:
  0.0 122.7 jit_solution(5983928902052644536)
XLA Ops:
  6.5 0.7 all-gather.2.cloned.1.call-update
  7.3 0.7 multiply_bitcast_fusion
  8.1 0.6 slice_reduce_fusion.1
  10.1 1.4 %reshape_squeeze.3 = bf16[2,64,4,4,128]{4,3,2,1,0:T(4,128)(2,1)S(1)} reshape(bf16[1,128,2048]{2,1,0:T(8,128)(2,1)} %param.9) | data formatting | bytes 1048576 | tf_op jit(solution)/shard_map/reshape;squeeze | solution.py:70
  11.8 49.7 %all-gather.2.cloned.1.call-done = bf16[1,1024,2,512]{3,2,0,1:T(2,128)(2,1)} async-done(((bf16[1,128,2,512]{3,2,0,1:T(2,128)(2,1)}), bf16[1,1024,2,512]{3,2,0,1:T(2,128)(2,1)}) %all-gather.2.cloned.1.call-update) | async-done | bytes 2097168 | tf_op jit(solution)/shard_map/all_gather | solution.py:84
  61.5 1.1 broadcast_in_dim.45
  62.6 37.0 %while.43 = (s32[]{:T(128)}, bf16[1024,2,512]{2,1,0:T(2,128)(2,1)S(1)}, bf16[1024,2,512]{2,1,0:T(2,128)(2,1)}, s32[16]{0:T(128)S(1)}, s32[]{:T(128)}, /*index=5*/s32[1]{0:T(128)}, s32[]{:T(128)}, s32[]{:T(128)}, s32[]{:T(128)}) while((s32[]{:T(128)}, bf16[1024,2,512]{2,1,0:T(2,128)(2,1)S(1)}, bf16[1024,2,512]{2,1,0:T(2,128)(2,1)}, ...), condition=%wide.region_2.3_spmd, body=%wide.region_1.2_spmd.sunk | while | flops 10 | bytes 262349 | solution.py:92
  62.6 0.6 dynamic_slice.32
  63.9 1.0 dynamic-slice_dynamic-update-slice_fusion.2
  66.2 1.0 dynamic-slice_dynamic-update-slice_fusion.2
  68.5 1.0 dynamic-slice_dynamic-update-slice_fusion.2
  70.8 1.0 dynamic-slice_dynamic-update-slice_fusion.2
  73.1 1.0 dynamic-slice_dynamic-update-slice_fusion.2
  75.4 1.0 dynamic-slice_dynamic-update-slice_fusion.2
  77.8 1.0 dynamic-slice_dynamic-update-slice_fusion.2
  80.1 1.0 dynamic-slice_dynamic-update-slice_fusion.2
  82.4 1.0 dynamic-slice_dynamic-update-slice_fusion.2
  84.7 1.0 dynamic-slice_dynamic-update-slice_fusion.2
  87.0 1.0 dynamic-slice_dynamic-update-slice_fusion.2
  89.3 1.0 dynamic-slice_dynamic-update-slice_fusion.2
  91.6 1.0 dynamic-slice_dynamic-update-slice_fusion.2
  93.9 1.0 dynamic-slice_dynamic-update-slice_fusion.2
  96.2 1.0 dynamic-slice_dynamic-update-slice_fusion.2
  98.5 1.0 dynamic-slice_dynamic-update-slice_fusion.2
  99.6 1.3 %copy-done = bf16[1024,2,512]{2,1,0:T(2,128)(2,1)} copy-done((bf16[1024,2,512]{2,1,0:T(2,128)(2,1)}, bf16[1024,2,512]{2,1,0:T(2,128)(2,1)S(1)}, u32[]{:S(2)}) %copy-start) | copy-done | bytes 2097176
  100.9 4.7 %copy.28 = bf16[1024,2,512]{0,2,1:T(8,128)(2,1)S(1)} copy(bf16[1024,2,512]{2,1,0:T(2,128)(2,1)} %copy-done) | data formatting | bytes 4194304
  105.7 2.6 %while.44 = (s32[]{:T(128)}, f32[4,256]{1,0:T(4,128)S(1)}, f32[4,256]{1,0:T(4,128)S(1)}, f32[4,256,128]{2,1,0:T(8,128)S(1)}, s32[]{:T(128)}, /*index=5*/s32[1,25...) while((s32[]{:T(128)}, f32[4,256]{1,0:T(4,128)S(1)}, ...), condition=%wide.region_6.7_spmd.clone, body=%wide.region_3.6_spmd.clone.sunk | while | flops 275646976 | bytes 11343043 | solution.py:49
  107.2 1.1 convolution_add_fusion.4
  108.8 5.1 %while.45 = (s32[]{:T(128)}, f32[4,256]{1,0:T(4,128)S(1)}, f32[4,256]{1,0:T(4,128)S(1)}, f32[4,256,128]{2,1,0:T(8,128)S(1)}, s32[]{:T(128)}, /*index=5*/s32[1,25...) while((s32[]{:T(128)}, f32[4,256]{1,0:T(4,128)S(1)}, ...), condition=%wide.region_11.12_spmd.clone, body=%wide.region_8.11_spmd.clone.sunk | while | flops 275646976 | bytes 11343043 | solution.py:49
  110.2 1.1 convolution_add_fusion.5
  112.8 1.1 convolution_add_fusion.5
  114.7 1.2 convert_element_type.22
  (59 shorter events, 15.4 us)
Async XLA Ops:
  6.5 55.0 %all-gather.2.cloned.1.call-start = ((), (), s32[]{:S(2)}) async-start(), calls=%async_computation | async-start | bytes 2359296 | tf_op jit(solution)/shard_map/all_gather | solution.py:84
  11.5 51.1 %copy-start.1 = (s32[1,16]{1,0:T(1,128)S(1)}, s32[1,16]{1,0:T(1,128)}, u32[]{:S(2)}) copy-start(s32[1,16]{1,0:T(1,128)} %param.11) | copy-start | bytes 196
  99.6 1.4 %copy-start = (bf16[1024,2,512]{2,1,0:T(2,128)(2,1)}, bf16[1024,2,512]{2,1,0:T(2,128)(2,1)S(1)}, u32[]{:S(2)}) copy-start(bf16[1024,2,512]{2,1,0:T(2,128)(2,1)S(1)} %get-tuple-element.255) | copy-start | bytes 6291460
Sparse Core Ops, SparseCore 0:
  9.5 51.9 all-gather.1
where the time goes:
time: 123 us
  waiting for transfers between devices  50.4 us (41%)
  local copies, waits for them, and re-layouts  37.4 us (30%)
  between operations  14.9 us (12%)
  loops' own time  10.7 us (9%)
  matrix products  5 us (4%)
  other arithmetic  4.33 us (4%)
    all_gather x1, waiting for transfers between devices, per_device(): piece_rows = lax.all_gather(keyvals, 'ctx', axis=1, tiled=True)[0]  49.7 us
    dynamic_update_slice x16, local copies, waits for them, and re-layouts, place_one(): lax.dynamic_update_slice_in_dim(current, rows, position_span * span_rows, 0)  16.3 us
    another operation x1, loops' own time, per_device(): buffer = lax.fori_loop(0, span_total, place_one, empty)  10.4 us
    dynamic_slice x16, local copies, waits for them, and re-layouts, place_one(): position_span = lax.dynamic_index_in_dim(span_table, index, 0, False)  10.2 us
    unnamed x5, local copies, waits for them, and re-layouts  6.08 us
    dot_general x3, matrix products, visit(): jnp.einsum('hrn,nhd->hrd', weights.astype(jnp.bfloat16), value_block, pre...  3.29 us
  transfers between devices with their start and end apart: 1, of which 1 were waited for; matrix products, arithmetic and copies ran while one was open for 3% of the time, Pallas kernels for 0%

commit v1 on v0

v1 whole, which is shorter than its diff:
```python
import functools
import math

import jax
import jax.numpy as jnp
from jax import lax
from jax.experimental import pallas as pl
from jax.experimental.pallas import tpu as pltpu
from jax.sharding import PartitionSpec as P

KV_HEADS = 4
GROUP = 4
HEAD_DIM = 128
NT = (((1,), (1,)), ((), ()))
TN = (((0,), (0,)), ((), ()))


def ring_order(count):
    return [i for i in range(count) if i % 2 == 0] + [i for i in reversed(range(count)) if i % 2]


def ring_member(place, count):
    half = (count + 1) // 2
    return jnp.where(place < half, 2 * place, 2 * (count - 1 - place) + 1)


def ring_place(member, count):
    return jnp.where(member % 2 == 0, member // 2, count - 1 - member // 2)


def attend(count, shifts, span_ref, q_ref, *refs):
    own_early, own_late = refs[0], refs[1]
    chunk_refs = refs[2 : 2 + 2 * len(shifts)]
    out_ref, q_scr, acc, top, total = refs[2 + 2 * len(shifts) :]
    rows = own_early.shape[0]
    width = KV_HEADS * HEAD_DIM
    slot_rows = GROUP * rows
    scale = math.log2(math.e) / math.sqrt(HEAD_DIM)
    me = lax.axis_index("ctx")
    place = ring_place(me, count)
    own_span = span_ref[0, 2 * me]

    for slot in range(2):
        for j in range(KV_HEADS):
            for g in range(GROUP):
                h = j * GROUP + g
                q_scr[slot, j, g * rows : (g + 1) * rows, :] = q_ref[
                    slot * rows : (slot + 1) * rows, h * HEAD_DIM : (h + 1) * HEAD_DIM
                ]

    def key(piece, j):
        return piece[:, j * HEAD_DIM : (j + 1) * HEAD_DIM]

    def value(piece, j):
        return piece[:, width + j * HEAD_DIM : width + (j + 1) * HEAD_DIM]

    def scores(k, q):
        return lax.dot_general(k, q, NT, preferred_element_type=jnp.float32) * scale

    def first(slot, j, s, v):
        new = jnp.max(s, axis=0, keepdims=True)
        p = jnp.exp2(s - new)
        top[slot, j] = new
        total[slot, j] = jnp.sum(p, axis=0, keepdims=True)
        acc[slot, j] = lax.dot_general(
            v, p.astype(jnp.bfloat16), TN, preferred_element_type=jnp.float32
        )

    def later(slot, j, s, v):
        old = top[slot, j]
        new = jnp.maximum(old, jnp.max(s, axis=0, keepdims=True))
        shrink = jnp.exp2(old - new)
        p = jnp.exp2(s - new)
        top[slot, j] = new
        total[slot, j] = total[slot, j] * shrink + jnp.sum(p, axis=0, keepdims=True)
        acc[slot, j] = acc[slot, j] * shrink + lax.dot_general(
            v, p.astype(jnp.bfloat16), TN, preferred_element_type=jnp.float32
        )

    key_row = lax.broadcasted_iota(jnp.int32, (rows, slot_rows), 0)
    query_row = lax.broadcasted_iota(jnp.int32, (rows, slot_rows), 1) % rows
    causal = key_row <= query_row
    early, late = own_early[...], own_late[...]
    for j in range(KV_HEADS):
        s = jnp.where(causal, scores(key(early, j), q_scr[0, j]), -1e30)
        first(0, j, s, value(early, j))
        s = jnp.where(causal, scores(key(late, j), q_scr[1, j]), -1e30)
        s = jnp.concatenate([scores(key(early, j), q_scr[1, j]), s], axis=0)
        first(1, j, s, jnp.concatenate([value(early, j), value(late, j)], axis=0))

    for i, shift in enumerate(shifts):
        other = ring_member((place + shift + count) % count, count)
        before = span_ref[0, 2 * other] < own_span
        slot = jnp.where(before, 0, 1)
        early, late = chunk_refs[2 * i][...], chunk_refs[2 * i + 1][...]
        picked = jnp.where(before, early, late)
        for j in range(KV_HEADS):
            later(1, j, scores(key(early, j), q_scr[1, j]), value(early, j))
        for j in range(KV_HEADS):
            later(slot, j, scores(key(picked, j), q_scr[slot, j]), value(picked, j))

    for slot in range(2):
        for j in range(KV_HEADS):
            result = (acc[slot, j] / total[slot, j]).T.astype(jnp.bfloat16)
            for g in range(GROUP):
                h = j * GROUP + g
                out_ref[
                    slot * rows : (slot + 1) * rows, h * HEAD_DIM : (h + 1) * HEAD_DIM
                ] = result[g * rows : (g + 1) * rows]


def per_device(queries, keyvals, span_ids):
    count = lax.axis_size("ctx")
    tok_rows = queries.shape[1]
    rows = tok_rows // 2
    features = queries.shape[2]
    kv_width = 2 * KV_HEADS * HEAD_DIM
    order = ring_order(count)
    ahead = [(order[i], order[(i + 1) % count]) for i in range(count)]
    back = [(b, a) for a, b in ahead]

    own = [keyvals[0, s * rows : (s + 1) * rows].reshape(rows, kv_width) for s in range(2)]
    shifts, chunks = [], []
    up, down = own, own
    for step in range(1, (count - 1) // 2 + 1):
        up = [lax.ppermute(up[0], "ctx", ahead), lax.ppermute(up[1], "ctx", ahead)]
        down = [lax.ppermute(down[0], "ctx", back), lax.ppermute(down[1], "ctx", back)]
        chunks += [up, down]
        shifts += [-step, step]
    if count % 2 == 0 and count > 1:
        chunks.append([lax.ppermute(up[0], "ctx", ahead), lax.ppermute(down[1], "ctx", back)])
        shifts.append(-(count // 2))
    pieces = own + [piece for chunk in chunks for piece in chunk]
    vmem = pl.BlockSpec(memory_space=pltpu.VMEM)
    slot_rows = GROUP * rows
    out = pl.pallas_call(
        functools.partial(attend, count, tuple(shifts)),
        out_shape=jax.ShapeDtypeStruct((tok_rows, features), jnp.bfloat16),
        in_specs=[pl.BlockSpec(memory_space=pltpu.SMEM), vmem] + [vmem] * len(pieces),
        out_specs=vmem,
        scratch_shapes=[
            pltpu.VMEM((2, KV_HEADS, slot_rows, HEAD_DIM), jnp.bfloat16),
            pltpu.VMEM((2, KV_HEADS, HEAD_DIM, slot_rows), jnp.float32),
            pltpu.VMEM((2, KV_HEADS, 1, slot_rows), jnp.float32),
            pltpu.VMEM((2, KV_HEADS, 1, slot_rows), jnp.float32),
        ],
        compiler_params=pltpu.CompilerParams(vmem_limit_bytes=48 * 1024 * 1024),
    )(span_ids, queries[0], *pieces)
    return out[None]


def solution(mesh):
    in_specs = (P("fsdp", "ctx", None), P("fsdp", "ctx", None, None), P("fsdp", None))
    out_specs = P("fsdp", "ctx", None)
    return jax.shard_map(
        per_device, mesh=mesh, in_specs=in_specs, out_specs=out_specs, check_vma=False
    )
```

time: 123 us -> 34.2 us (0.28)
  waiting for transfers between devices: 50.4 us -> 11.5 us
  local copies, waits for them, and re-layouts: 37.4 us -> 1.25 us
  starting transfers between devices: 0.01 us -> 15.8 us
  between operations: 14.9 us -> 0.05 us
  loops' own time: 10.7 us -> 0 us
  Pallas kernels: 0 us -> 5.48 us
  matrix products: 5 us -> 0 us
  other arithmetic: 4.33 us -> 0 us
    all_gather x1 -> x0, waiting for transfers between devices: 49.7 us -> none  [per_device(): piece_rows = lax.all_gather(keyvals, 'ctx', axis=1, tiled=True)[0]]
    dynamic_update_slice x16 -> x0, local copies, waits for them, and re-layouts: 16.3 us -> none  [place_one(): lax.dynamic_update_slice_in_dim(current, rows, position_span * span_rows, 0)]
    ppermute x0 -> x14, starting transfers between devices: none -> 15.8 us  [the longest x6 11.2 us: per_device(): up = [lax.ppermute(up[0], 'ctx', ahead), lax.ppermute(up[1], 'ctx', ahead)]]
    ppermute x0 -> x14, waiting for transfers between devices: none -> 11.5 us  [the longest x3 5.88 us: per_device(): lax.ppermute(down[0], 'ctx', back)]
    another operation x3 -> x0, loops' own time: 10.7 us -> none  [the longest x1 10.4 us: per_device(): buffer = lax.fori_loop(0, span_total, place_one, empty)]
    dynamic_slice x16 -> x0, local copies, waits for them, and re-layouts: 10.2 us -> none  [place_one(): position_span = lax.dynamic_index_in_dim(span_table, index, 0, False)]
    unnamed x5 -> x6, local copies, waits for them, and re-layouts: 6.08 us -> 0.04 us
    pallas_call x0 -> x1, Pallas kernels: none -> 5.48 us  [per_device(): pl.pallas_call(functools.partial(attend, count, tuple(shifts)), out_shape...]
  transfers between devices with their start and end apart: 1 -> 14, of which waited for: 1 -> 7; matrix products, arithmetic and copies ran while one was open for 3% -> 0% of each run, Pallas kernels for 0% -> 0%
where the time goes in v1:
time: 34.2 us; the launch traced here: 34.1 us
  starting transfers between devices  15.8 us (46%)
  waiting for transfers between devices  11.5 us (34%)
  Pallas kernels  5.48 us (16%)
  local copies, waits for them, and re-layouts  1.25 us (4%)
    ppermute x6, starting transfers between devices, per_device(): up = [lax.ppermute(up[0], 'ctx', ahead), lax.ppermute(up[1], 'ctx', ahead)]  11.2 us
    ppermute x3, waiting for transfers between devices, per_device(): lax.ppermute(down[0], 'ctx', back)  5.88 us
    pallas_call x1, Pallas kernels, per_device(): pl.pallas_call(functools.partial(attend, count, tuple(shifts)), out_shape...  5.48 us
    ppermute x3, starting transfers between devices, per_device(): lax.ppermute(down[0], 'ctx', back)  2.05 us
    ppermute x1, waiting for transfers between devices, per_device(): lax.ppermute(up[0], 'ctx', ahead)  1.95 us
    ppermute x4, waiting for transfers between devices, per_device(): lax.ppermute(down[1], 'ctx', back)  1.89 us
    ppermute x1, starting transfers between devices, per_device(): lax.ppermute(up[0], 'ctx', ahead)  1.82 us
    ppermute x6, waiting for transfers between devices, per_device(): up = [lax.ppermute(up[0], 'ctx', ahead), lax.ppermute(up[1], 'ctx', ahead)]  1.78 us
  transfers between devices with their start and end apart: 14, of which 7 were waited for; matrix products, arithmetic and copies ran while one was open for 0% of the time, Pallas kernels for 0%

profile of v1, /device:TPU:0, one launch (start us, length us, event | category | flops | bytes accessed | tf_op | source)
XLA Modules:
  0.0 34.1 jit_solution(16645025874429531349)
XLA Ops:
  0.0 1.2 %fusion = (bf16[1,64,2,512]{3,2,1,0:T(2,128)(2,1)S(1)}, bf16[1,64,2,512]{3,2,1,0:T(2,128)(2,1)S(1)}) fusion(bf16[1,128,2,512]{3,2,1,0:T(2,128)(2,1)} %param.4), kind=kLoop, calls=%fused_computation | loop fusion | bytes 524288 | tf_op jit(solution)/shard_map/slice | solution.py:122
  1.2 3.1 %collective-permute-start = (bf16[64,1024]{1,0:T(8,128)(2,1)S(1)}, bf16[64,1024]{1,0:T(8,128)(2,1)S(1)}, u32[]{:S(2)}, u32[]{:S(2)}) collective-permute-start(bf16[64,1024]{1,0:T(8,128)(2,1)S(1)} %bitcast.9), channel_id=1, source_target_pairs={{0,2},{2,4},{4,6},{6,7},{7,5},{5,3},{3,1},{1,0},{8,10},{10,12},{12... | collective-permute-start | bytes 393224 | tf_op jit(solution)/shard_map/ppermute | solution.py:126
  4.3 0.0 copy-start.1
  4.3 0.1 collective-permute-start.3
  4.4 2.0 %collective-permute-start.2 = (bf16[64,1024]{1,0:T(8,128)(2,1)S(1)}, bf16[64,1024]{1,0:T(8,128)(2,1)S(1)}, u32[]{:S(2)}, u32[]{:S(2)}) collective-permute-start(bf16[64,1024]{1,0:T(8,128)(2,1)S(1)} %bitcast.10), channel_id=1, source_target_pairs={{2,0},{4,2},{6,4},{7,6},{5,7},{3,5},{1,3},{0,1},{10,8},{12,10},{14... | collective-permute-start | bytes 393224 | tf_op jit(solution)/shard_map/ppermute | solution.py:127
  6.4 0.1 collective-permute-start.1
  6.5 1.7 %collective-permute-done.refs_2_ = bf16[64,1024]{1,0:T(8,128)(2,1)S(1)} collective-permute-done((bf16[64,1024]{1,0:T(8,128)(2,1)S(1)}, bf16[64,1024]{1,0:T(8,128)(2,1)S(1)}, u32[]{:S(2)}, u32[]{:S(2)}) %collective-permute-start) | collective-permute-done | bytes 131104 | tf_op jit(solution)/shard_map/ppermute | solution.py:126
  8.2 2.5 %collective-permute-start.4 = (bf16[64,1024]{1,0:T(8,128)(2,1)S(1)}, bf16[64,1024]{1,0:T(8,128)(2,1)S(1)}, u32[]{:S(2)}, u32[]{:S(2)}) collective-permute-start(bf16[64,1024]{1,0:T(8,128)(2,1)S(1)} %collective-permute-done.refs_2_), channel_id=1, source_target_pairs={{0,2},{2,4},{4,6},{6,7},{7,5},{5,3},{3,1},{1,0},{8,10},{10,12},{12... | collective-permute-start | bytes 393224 | tf_op jit(solution)/shard_map/ppermute | solution.py:126
  10.7 0.1 collective-permute-done.3.refs_5_
  10.8 0.0 collective-permute-start.7
  10.8 2.6 %collective-permute-done.2.refs_4_ = bf16[64,1024]{1,0:T(8,128)(2,1)S(1)} collective-permute-done((bf16[64,1024]{1,0:T(8,128)(2,1)S(1)}, bf16[64,1024]{1,0:T(8,128)(2,1)S(1)}, u32[]{:S(2)}, u32[]{:S(2)}) %collective-permute-start.2) | collective-permute-done | bytes 131104 | tf_op jit(solution)/shard_map/ppermute | solution.py:127
  13.4 0.0 collective-permute-start.6
  13.5 0.0 collective-permute-done.1.refs_3_
  13.5 2.0 %collective-permute-start.5 = (bf16[64,1024]{1,0:T(8,128)(2,1)S(1)}, bf16[64,1024]{1,0:T(8,128)(2,1)S(1)}, u32[]{:S(2)}, u32[]{:S(2)}) collective-permute-start(bf16[64,1024]{1,0:T(8,128)(2,1)S(1)} %collective-permute-done.1.refs_3_), channel_id=1, source_target_pairs={{0,2},{2,4},{4,6},{6,7},{7,5},{5,3},{3,1},{1,0},{8,10},{10,12},{12... | collective-permute-start | bytes 393224 | tf_op jit(solution)/shard_map/ppermute | solution.py:126
  15.5 0.0 collective-permute-done.4.refs_6_
  15.5 1.6 %collective-permute-start.8 = (bf16[64,1024]{1,0:T(8,128)(2,1)S(1)}, bf16[64,1024]{1,0:T(8,128)(2,1)S(1)}, u32[]{:S(2)}, u32[]{:S(2)}) collective-permute-start(bf16[64,1024]{1,0:T(8,128)(2,1)S(1)} %collective-permute-done.4.refs_6_), channel_id=1, source_target_pairs={{0,2},{2,4},{4,6},{6,7},{7,5},{5,3},{3,1},{1,0},{8,10},{10,12},{12... | collective-permute-start | bytes 393224 | tf_op jit(solution)/shard_map/ppermute | solution.py:126
  17.1 0.0 collective-permute-done.7.refs_9_
  17.1 0.4 %collective-permute-start.11 = (bf16[64,1024]{1,0:T(8,128)(2,1)S(1)}, bf16[64,1024]{1,0:T(8,128)(2,1)S(1)}, u32[]{:S(2)}, u32[]{:S(2)}) collective-permute-start(bf16[64,1024]{1,0:T(8,128)(2,1)S(1)} %collective-permute-done.7.refs_9_), channel_id=1, source_target_pairs={{2,0},{4,2},{6,4},{7,6},{5,7},{3,5},{1,3},{0,1},{10,8},{12,10},{14... | collective-permute-start | bytes 393224 | tf_op jit(solution)/shard_map/ppermute | solution.py:127
  17.5 2.3 %collective-permute-done.6.refs_8_ = bf16[64,1024]{1,0:T(8,128)(2,1)S(1)} collective-permute-done((bf16[64,1024]{1,0:T(8,128)(2,1)S(1)}, bf16[64,1024]{1,0:T(8,128)(2,1)S(1)}, u32[]{:S(2)}, u32[]{:S(2)}) %collective-permute-start.6) | collective-permute-done | bytes 131104 | tf_op jit(solution)/shard_map/ppermute | solution.py:127
  19.8 0.1 collective-permute-start.10
  19.8 0.0 collective-permute-done.5.refs_7_
  19.8 2.0 %collective-permute-start.9 = (bf16[64,1024]{1,0:T(8,128)(2,1)S(1)}, bf16[64,1024]{1,0:T(8,128)(2,1)S(1)}, u32[]{:S(2)}, u32[]{:S(2)}) collective-permute-start(bf16[64,1024]{1,0:T(8,128)(2,1)S(1)} %collective-permute-done.5.refs_7_), channel_id=1, source_target_pairs={{0,2},{2,4},{4,6},{6,7},{7,5},{5,3},{3,1},{1,0},{8,10},{10,12},{12... | collective-permute-start | bytes 393224 | tf_op jit(solution)/shard_map/ppermute | solution.py:126
  21.8 0.0 collective-permute-done.8.refs_10_
  21.8 1.8 %collective-permute-start.12 = (bf16[64,1024]{1,0:T(8,128)(2,1)S(1)}, bf16[64,1024]{1,0:T(8,128)(2,1)S(1)}, u32[]{:S(2)}, u32[]{:S(2)}) collective-permute-start(bf16[64,1024]{1,0:T(8,128)(2,1)S(1)} %collective-permute-done.8.refs_10_), channel_id=1, source_target_pairs={{0,2},{2,4},{4,6},{6,7},{7,5},{5,3},{3,1},{1,0},{8,10},{10,12},{12... | collective-permute-start | bytes 393224 | tf_op jit(solution)/shard_map/ppermute | solution.py:131
  23.6 0.0 collective-permute-done.11.refs_13_
  23.6 0.2 collective-permute-start.13
  23.9 1.0 %collective-permute-done.10.refs_12_ = bf16[64,1024]{1,0:T(8,128)(2,1)S(1)} collective-permute-done((bf16[64,1024]{1,0:T(8,128)(2,1)S(1)}, bf16[64,1024]{1,0:T(8,128)(2,1)S(1)}, u32[]{:S(2)}, u32[]{:S(2)}) %collective-permute-start.10) | collective-permute-done | bytes 131104 | tf_op jit(solution)/shard_map/ppermute | solution.py:127
  24.8 0.0 collective-permute-done.9.refs_11_
  24.8 2.0 %collective-permute-done.12.refs_14_ = bf16[64,1024]{1,0:T(8,128)(2,1)S(1)} collective-permute-done((bf16[64,1024]{1,0:T(8,128)(2,1)S(1)}, bf16[64,1024]{1,0:T(8,128)(2,1)S(1)}, u32[]{:S(2)}, u32[]{:S(2)}) %collective-permute-start.12) | collective-permute-done | bytes 131104 | tf_op jit(solution)/shard_map/ppermute | solution.py:131
  26.8 1.8 %collective-permute-done.13.refs_15_ = bf16[64,1024]{1,0:T(8,128)(2,1)S(1)} collective-permute-done((bf16[64,1024]{1,0:T(8,128)(2,1)S(1)}, bf16[64,1024]{1,0:T(8,128)(2,1)S(1)}, u32[]{:S(2)}, u32[]{:S(2)}) %collective-permute-start.13) | collective-permute-done | bytes 131104 | tf_op jit(solution)/shard_map/ppermute | solution.py:131
  28.6 0.0 copy-done.1
  28.6 5.5 %shard_map.37 = bf16[128,2048]{1,0:T(8,128)(2,1)} custom-call(s32[1,16]{1,0:T(1,128)S(1)} %copy-done.1, bf16[128,2048]{1,0:T(8,128)(2,1)S(1)} %bitcast.8, bf16[64,1024]{1,0:T(8,128)(2,1)S(1)} %bitcast.11, bf16[64,1024]{1,0:T(8,128)(2,1)S(1)} %bitcast.14, bf16[64,1024]{1,0:T(8,128)(2,1)S(1)} %collective-permute-done.refs_2_, ...), custom_call_target="tpu_custom_call" | custom-call | tf_op jit(solution)/shard_map/pallas_call | solution.py:136
  (4 shorter events, 0.0 us)
Async XLA Ops:
  0.0 28.6 %copy-start = (bf16[1,128,2048]{2,1,0:T(8,128)(2,1)S(1)}, bf16[1,128,2048]{2,1,0:T(8,128)(2,1)}, u32[]{:S(2)}) copy-start(bf16[1,128,2048]{2,1,0:T(8,128)(2,1)} %param.3) | copy-start | bytes 1572868
  1.2 7.0 %collective-permute-start = (bf16[64,1024]{1,0:T(8,128)(2,1)S(1)}, bf16[64,1024]{1,0:T(8,128)(2,1)S(1)}, u32[]{:S(2)}, u32[]{:S(2)}) collective-permute-start(bf16[64,1024]{1,0:T(8,128)(2,1)S(1)} %bitcast.9), channel_id=1, source_target_pairs={{0,2},{2,4},{4,6},{6,7},{7,5},{5,3},{3,1},{1,0},{8,10},{10,12},{12... | collective-permute-start | bytes 393224 | tf_op jit(solution)/shard_map/ppermute | solution.py:126
  4.3 24.3 %copy-start.1 = (s32[1,16]{1,0:T(1,128)S(1)}, s32[1,16]{1,0:T(1,128)}, u32[]{:S(2)}) copy-start(s32[1,16]{1,0:T(1,128)} %span_ref.1) | copy-start | bytes 196
  4.3 6.4 %collective-permute-start.3 = (bf16[64,1024]{1,0:T(8,128)(2,1)S(1)}, bf16[64,1024]{1,0:T(8,128)(2,1)S(1)}, u32[]{:S(2)}, u32[]{:S(2)}) collective-permute-start(bf16[64,1024]{1,0:T(8,128)(2,1)S(1)} %bitcast.12), channel_id=1, source_target_pairs={{2,0},{4,2},{6,4},{7,6},{5,7},{3,5},{1,3},{0,1},{10,8},{12,10},{14... | collective-permute-start | bytes 393224 | tf_op jit(solution)/shard_map/ppermute | solution.py:127
  4.4 9.0 %collective-permute-start.2 = (bf16[64,1024]{1,0:T(8,128)(2,1)S(1)}, bf16[64,1024]{1,0:T(8,128)(2,1)S(1)}, u32[]{:S(2)}, u32[]{:S(2)}) collective-permute-start(bf16[64,1024]{1,0:T(8,128)(2,1)S(1)} %bitcast.10), channel_id=1, source_target_pairs={{2,0},{4,2},{6,4},{7,6},{5,7},{3,5},{1,3},{0,1},{10,8},{12,10},{14... | collective-permute-start | bytes 393224 | tf_op jit(solution)/shard_map/ppermute | solution.py:127
  6.4 7.1 %collective-permute-start.1 = (bf16[64,1024]{1,0:T(8,128)(2,1)S(1)}, bf16[64,1024]{1,0:T(8,128)(2,1)S(1)}, u32[]{:S(2)}, u32[]{:S(2)}) collective-permute-start(bf16[64,1024]{1,0:T(8,128)(2,1)S(1)} %bitcast.13), channel_id=1, source_target_pairs={{0,2},{2,4},{4,6},{6,7},{7,5},{5,3},{3,1},{1,0},{8,10},{10,12},{12... | collective-permute-start | bytes 393224 | tf_op jit(solution)/shard_map/ppermute | solution.py:126
  8.2 7.2 %collective-permute-start.4 = (bf16[64,1024]{1,0:T(8,128)(2,1)S(1)}, bf16[64,1024]{1,0:T(8,128)(2,1)S(1)}, u32[]{:S(2)}, u32[]{:S(2)}) collective-permute-start(bf16[64,1024]{1,0:T(8,128)(2,1)S(1)} %collective-permute-done.refs_2_), channel_id=1, source_target_pairs={{0,2},{2,4},{4,6},{6,7},{7,5},{5,3},{3,1},{1,0},{8,10},{10,12},{12... | collective-permute-start | bytes 393224 | tf_op jit(solution)/shard_map/ppermute | solution.py:126
  10.8 6.3 %collective-permute-start.7 = (bf16[64,1024]{1,0:T(8,128)(2,1)S(1)}, bf16[64,1024]{1,0:T(8,128)(2,1)S(1)}, u32[]{:S(2)}, u32[]{:S(2)}) collective-permute-start(bf16[64,1024]{1,0:T(8,128)(2,1)S(1)} %collective-permute-done.3.refs_5_), channel_id=1, source_target_pairs={{2,0},{4,2},{6,4},{7,6},{5,7},{3,5},{1,3},{0,1},{10,8},{12,10},{14... | collective-permute-start | bytes 393224 | tf_op jit(solution)/shard_map/ppermute | solution.py:127
  13.4 6.3 %collective-permute-start.6 = (bf16[64,1024]{1,0:T(8,128)(2,1)S(1)}, bf16[64,1024]{1,0:T(8,128)(2,1)S(1)}, u32[]{:S(2)}, u32[]{:S(2)}) collective-permute-start(bf16[64,1024]{1,0:T(8,128)(2,1)S(1)} %collective-permute-done.2.refs_4_), channel_id=1, source_target_pairs={{2,0},{4,2},{6,4},{7,6},{5,7},{3,5},{1,3},{0,1},{10,8},{12,10},{14... | collective-permute-start | bytes 393224 | tf_op jit(solution)/shard_map/ppermute | solution.py:127
  13.5 6.4 %collective-permute-start.5 = (bf16[64,1024]{1,0:T(8,128)(2,1)S(1)}, bf16[64,1024]{1,0:T(8,128)(2,1)S(1)}, u32[]{:S(2)}, u32[]{:S(2)}) collective-permute-start(bf16[64,1024]{1,0:T(8,128)(2,1)S(1)} %collective-permute-done.1.refs_3_), channel_id=1, source_target_pairs={{0,2},{2,4},{4,6},{6,7},{7,5},{5,3},{3,1},{1,0},{8,10},{10,12},{12... | collective-permute-start | bytes 393224 | tf_op jit(solution)/shard_map/ppermute | solution.py:126
  15.5 6.4 %collective-permute-start.8 = (bf16[64,1024]{1,0:T(8,128)(2,1)S(1)}, bf16[64,1024]{1,0:T(8,128)(2,1)S(1)}, u32[]{:S(2)}, u32[]{:S(2)}) collective-permute-start(bf16[64,1024]{1,0:T(8,128)(2,1)S(1)} %collective-permute-done.4.refs_6_), channel_id=1, source_target_pairs={{0,2},{2,4},{4,6},{6,7},{7,5},{5,3},{3,1},{1,0},{8,10},{10,12},{12... | collective-permute-start | bytes 393224 | tf_op jit(solution)/shard_map/ppermute | solution.py:126
  17.1 6.6 %collective-permute-start.11 = (bf16[64,1024]{1,0:T(8,128)(2,1)S(1)}, bf16[64,1024]{1,0:T(8,128)(2,1)S(1)}, u32[]{:S(2)}, u32[]{:S(2)}) collective-permute-start(bf16[64,1024]{1,0:T(8,128)(2,1)S(1)} %collective-permute-done.7.refs_9_), channel_id=1, source_target_pairs={{2,0},{4,2},{6,4},{7,6},{5,7},{3,5},{1,3},{0,1},{10,8},{12,10},{14... | collective-permute-start | bytes 393224 | tf_op jit(solution)/shard_map/ppermute | solution.py:127
  19.8 5.1 %collective-permute-start.10 = (bf16[64,1024]{1,0:T(8,128)(2,1)S(1)}, bf16[64,1024]{1,0:T(8,128)(2,1)S(1)}, u32[]{:S(2)}, u32[]{:S(2)}) collective-permute-start(bf16[64,1024]{1,0:T(8,128)(2,1)S(1)} %collective-permute-done.6.refs_8_), channel_id=1, source_target_pairs={{2,0},{4,2},{6,4},{7,6},{5,7},{3,5},{1,3},{0,1},{10,8},{12,10},{14... | collective-permute-start | bytes 393224 | tf_op jit(solution)/shard_map/ppermute | solution.py:127
  19.8 5.0 %collective-permute-start.9 = (bf16[64,1024]{1,0:T(8,128)(2,1)S(1)}, bf16[64,1024]{1,0:T(8,128)(2,1)S(1)}, u32[]{:S(2)}, u32[]{:S(2)}) collective-permute-start(bf16[64,1024]{1,0:T(8,128)(2,1)S(1)} %collective-permute-done.5.refs_7_), channel_id=1, source_target_pairs={{0,2},{2,4},{4,6},{6,7},{7,5},{5,3},{3,1},{1,0},{8,10},{10,12},{12... | collective-permute-start | bytes 393224 | tf_op jit(solution)/shard_map/ppermute | solution.py:126
  21.8 5.0 %collective-permute-start.12 = (bf16[64,1024]{1,0:T(8,128)(2,1)S(1)}, bf16[64,1024]{1,0:T(8,128)(2,1)S(1)}, u32[]{:S(2)}, u32[]{:S(2)}) collective-permute-start(bf16[64,1024]{1,0:T(8,128)(2,1)S(1)} %collective-permute-done.8.refs_10_), channel_id=1, source_target_pairs={{0,2},{2,4},{4,6},{6,7},{7,5},{5,3},{3,1},{1,0},{8,10},{10,12},{12... | collective-permute-start | bytes 393224 | tf_op jit(solution)/shard_map/ppermute | solution.py:131
  23.6 5.0 %collective-permute-start.13 = (bf16[64,1024]{1,0:T(8,128)(2,1)S(1)}, bf16[64,1024]{1,0:T(8,128)(2,1)S(1)}, u32[]{:S(2)}, u32[]{:S(2)}) collective-permute-start(bf16[64,1024]{1,0:T(8,128)(2,1)S(1)} %collective-permute-done.11.refs_13_), channel_id=1, source_target_pairs={{2,0},{4,2},{6,4},{7,6},{5,7},{3,5},{1,3},{0,1},{10,8},{12,10},{14... | collective-permute-start | bytes 393224 | tf_op jit(solution)/shard_map/ppermute | solution.py:131

commit v2 on v1

v2 whole, which is shorter than its diff:
```python
import functools
import math

import jax
import jax.numpy as jnp
from jax import lax
from jax.experimental import pallas as pl
from jax.experimental.pallas import tpu as pltpu
from jax.sharding import PartitionSpec as P

KV_HEADS = 4
GROUP = 4
HEAD_DIM = 128
WIDTH = KV_HEADS * HEAD_DIM
NT = (((1,), (1,)), ((), ()))
TN = (((0,), (0,)), ((), ()))


def ring_order(count):
    return [i for i in range(count) if i % 2 == 0] + [i for i in reversed(range(count)) if i % 2]


def ring_member(place, count):
    half = (count + 1) // 2
    return jnp.where(place < half, 2 * place, 2 * (count - 1 - place) + 1)


def ring_place(member, count):
    return jnp.where(member % 2 == 0, member // 2, count - 1 - member // 2)


def key(piece, j):
    return piece[:, j * HEAD_DIM : (j + 1) * HEAD_DIM]


def value(piece, j):
    return piece[:, WIDTH + j * HEAD_DIM : WIDTH + (j + 1) * HEAD_DIM]


def attend(count, shifts, begin, end, span_ref, q_ref, *refs):
    refs = list(refs)
    chunks = [(refs.pop(0), refs.pop(0)) for _ in range(len(shifts) + begin)]
    if not begin:
        top_in, total_in, acc_in = refs.pop(0), refs.pop(0), refs.pop(0)
    if end:
        out_ref = refs.pop(0)
    else:
        top_out, total_out, acc_out = refs
    rows = chunks[0][0].shape[0]
    slot_rows = GROUP * rows
    scale = math.log2(math.e) / math.sqrt(HEAD_DIM)
    me = lax.axis_index("ctx")
    place = ring_place(me, count)
    table = span_ref[...].astype(jnp.float32)
    lane = lax.broadcasted_iota(jnp.int32, table.shape, 1)

    def span_of(member):
        return jnp.sum(jnp.where(lane == 2 * member, table, 0.0))


    def queries(slot, j):
        start = slot * rows if isinstance(slot, int) else pl.multiple_of(slot * rows, rows)
        return jnp.concatenate(
            [
                q_ref[pl.ds(start, rows), (j * GROUP + g) * HEAD_DIM : (j * GROUP + g + 1) * HEAD_DIM]
                for g in range(GROUP)
            ],
            axis=0,
        )

    def weigh(v, p):
        return lax.dot_general(v, p, TN, preferred_element_type=jnp.float32)

    def scores(k, q):
        return lax.dot_general(k, q, NT, preferred_element_type=jnp.float32) * scale

    heads = range(KV_HEADS)
    result = {}
    if begin:
        early, late = chunks.pop(0)
        key_row = lax.broadcasted_iota(jnp.int32, (rows, slot_rows), 0)
        query_row = lax.broadcasted_iota(jnp.int32, (rows, slot_rows), 1) % rows
        causal = key_row <= query_row
        for j in heads:
            q = queries(0, j)
            s = jnp.where(causal, scores(key(early, j), q), -1e30)
            new = jnp.max(s, axis=0, keepdims=True)
            p = jnp.exp2(s - new)
            result[0, j] = new, jnp.sum(p, axis=0, keepdims=True), weigh(value(early, j), p.astype(jnp.bfloat16))
            q = queries(1, j)
            k = jnp.concatenate([key(early, j), key(late, j)], axis=0)
            v = jnp.concatenate([value(early, j), value(late, j)], axis=0)
            s = scores(k, q)
            s = jnp.concatenate([s[:rows], jnp.where(causal, s[rows:], -1e30)], axis=0)
            new = jnp.max(s, axis=0, keepdims=True)
            p = jnp.exp2(s - new)
            result[1, j] = new, jnp.sum(p, axis=0, keepdims=True), weigh(v, p.astype(jnp.bfloat16))
    else:
        own_span = span_of(me)
        befores, slots, picked = [], [], []
        for shift, (early, late) in zip(shifts, chunks):
            other = ring_member((place + shift + count) % count, count)
            befores.append(span_of(other) < own_span)
            slots.append(jnp.where(befores[-1], 0, 1))
            picked.append(jnp.where(befores[-1], early[...], late[...]))
        n = len(shifts)
        full, part = {}, {}
        for j in heads:
            k = jnp.concatenate([key(early, j) for early, _ in chunks], axis=0)
            full[j] = scores(k, queries(1, j))
            part[j] = [scores(key(picked[i], j), queries(slots[i], j)) for i in range(n)]
        for j in heads:
            old = [top_in[0, j], top_in[1, j]]
            most = [jnp.max(s, axis=0, keepdims=True) for s in part[j]]
            new = [old[0], jnp.maximum(old[1], jnp.max(full[j], axis=0, keepdims=True))]
            for i in range(n):
                new[0] = jnp.maximum(new[0], jnp.where(befores[i], most[i], -1e30))
                new[1] = jnp.maximum(new[1], jnp.where(befores[i], -1e30, most[i]))
            p = jnp.exp2(full[j] - new[1])
            shrink = [jnp.exp2(old[slot] - new[slot]) for slot in range(2)]
            added = [total_in[0, j] * shrink[0], total_in[1, j] * shrink[1] + jnp.sum(p, axis=0, keepdims=True)]
            weights = [[], [p.astype(jnp.bfloat16)]]
            values = [[value(picked[i], j) for i in range(n)], [value(early, j) for early, _ in chunks]]
            values[1] += values[0]
            for i in range(n):
                p = jnp.exp2(part[j][i] - jnp.where(befores[i], new[0], new[1]))
                t = jnp.sum(p, axis=0, keepdims=True)
                p = p.astype(jnp.bfloat16)
                zero = jnp.zeros_like(p)
                added[0] = added[0] + jnp.where(befores[i], t, 0.0)
                added[1] = added[1] + jnp.where(befores[i], 0.0, t)
                weights[0].append(jnp.where(befores[i], p, zero))
                weights[1].append(jnp.where(befores[i], zero, p))
            for slot in range(2):
                update = weigh(
                    jnp.concatenate(values[slot], axis=0), jnp.concatenate(weights[slot], axis=0)
                )
                result[slot, j] = new[slot], added[slot], acc_in[slot, j] * shrink[slot] + update

    for (slot, j), (new, added, update) in result.items():
        if end:
            done = (update * (1.0 / added)).astype(jnp.bfloat16).T
            for g in range(GROUP):
                h = j * GROUP + g
                out_ref[
                    slot * rows : (slot + 1) * rows, h * HEAD_DIM : (h + 1) * HEAD_DIM
                ] = done[g * rows : (g + 1) * rows]
        else:
            top_out[slot, j] = new
            total_out[slot, j] = added
            acc_out[slot, j] = update


def fold(count, shifts, pieces, state, end, span_ids, queries):
    vmem = pl.BlockSpec(memory_space=pltpu.VMEM)
    tok_rows, features = queries.shape
    slot_rows = GROUP * (tok_rows // 2)
    begin = state is None
    state = [] if begin else list(state)
    if end:
        out_shape = jax.ShapeDtypeStruct((tok_rows, features), jnp.bfloat16)
    else:
        row = jax.ShapeDtypeStruct((2, KV_HEADS, 1, slot_rows), jnp.float32)
        out_shape = [row, row, jax.ShapeDtypeStruct((2, KV_HEADS, HEAD_DIM, slot_rows), jnp.float32)]
    keys = (len(pieces) // 2) * tok_rows
    return pl.pallas_call(
        functools.partial(attend, count, tuple(shifts), begin, end),
        out_shape=out_shape,
        in_specs=[vmem] * (2 + len(pieces) + len(state)),
        out_specs=vmem if end else [vmem] * 3,
        compiler_params=pltpu.CompilerParams(vmem_limit_bytes=32 * 1024 * 1024),
        cost_estimate=pl.CostEstimate(
            flops=2 * keys * features * tok_rows,
            bytes_accessed=2 * keys * 2 * WIDTH + 4 * tok_rows * features,
            transcendentals=keys * tok_rows * KV_HEADS * GROUP // 2,
        ),
    )(span_ids, queries, *pieces, *state)


def per_device(queries, keyvals, span_ids):
    count = lax.axis_size("ctx")
    rows = queries.shape[1] // 2
    order = ring_order(count)
    ahead = [(order[i], order[(i + 1) % count]) for i in range(count)]
    back = [(b, a) for a, b in ahead]

    flat = lax.optimization_barrier(keyvals[0].reshape(2 * rows, 2 * WIDTH))
    own = [flat[:rows], flat[rows:]]
    up, down = own, own
    last = count // 2
    held, state = ([], own), None
    for step in range(1, last + 1):
        if step > 1:
            state = fold(count, *held, state, False, span_ids, queries[0])
            up[0], *state = lax.optimization_barrier((up[0], *state))
            held = shifts, pieces
        if 2 * step < count:
            up = [lax.ppermute(piece, "ctx", ahead) for piece in up]
            down = [lax.ppermute(piece, "ctx", back) for piece in down]
            shifts, pieces = [-step, step], up + down
        else:
            shifts = [-step]
            pieces = [lax.ppermute(up[0], "ctx", ahead), lax.ppermute(down[1], "ctx", back)]
    if last:
        state = fold(count, *held, state, False, span_ids, queries[0])
        held = shifts, pieces
    return fold(count, *held, state, True, span_ids, queries[0])[None]


def solution(mesh):
    in_specs = (P("fsdp", "ctx", None), P("fsdp", "ctx", None, None), P("fsdp", None))
    out_specs = P("fsdp", "ctx", None)
    return jax.shard_map(
        per_device, mesh=mesh, in_specs=in_specs, out_specs=out_specs, check_vma=False
    )
```

time: 34.2 us -> 29.3 us (0.86)
  waiting for transfers between devices: 11.5 us -> 7.21 us
  Pallas kernels: 5.48 us -> 4.91 us
    ppermute x9 -> x12, waiting for transfers between devices: 7.66 us -> 5.19 us  [the longest x6 3.72 us: per_device(): up = [lax.ppermute(piece, 'ctx', ahead) for piece in up]]
    ppermute x1, waiting for transfers between devices: 1.95 us -> 0.12 us  [per_device(): lax.ppermute(up[0], 'ctx', ahead)]
    slice x1, local copies, waits for them, and re-layouts: 1.21 us -> 0.02 us  [per_device(): own = [flat[:rows], flat[rows:]]]
    unnamed x6 -> x5, local copies, waits for them, and re-layouts: 0.04 us -> 1.04 us
    ppermute x4 -> x1, starting transfers between devices: 0.72 us -> 0.12 us  [per_device(): lax.ppermute(down[1], 'ctx', back)]
    pallas_call x1 -> x5, Pallas kernels: 5.48 us -> 4.91 us  [fold(): pl.pallas_call(functools.partial(attend, count, tuple(shifts), begin, end...]
    ppermute x9 -> x12, starting transfers between devices: 13.3 us -> 13.8 us  [the longest x6 13.5 us: per_device(): up = [lax.ppermute(piece, 'ctx', ahead) for piece in up]]
    ppermute x4 -> x1, waiting for transfers between devices: 1.89 us -> 1.91 us  [per_device(): lax.ppermute(down[1], 'ctx', back)]
  transfers between devices with their start and end apart: 14 -> 14, of which waited for: 7 -> 8; matrix products, arithmetic and copies ran while one was open for 0% -> 0% of each run, Pallas kernels for 0% -> 11%
where the time goes in v2:
time: 29.3 us; the launch traced here: 29.2 us
  starting transfers between devices  15.9 us (54%)
  waiting for transfers between devices  7.21 us (25%)
  Pallas kernels  4.91 us (17%)
  local copies, waits for them, and re-layouts  1.06 us (4%)
    ppermute x6, starting transfers between devices, per_device(): up = [lax.ppermute(piece, 'ctx', ahead) for piece in up]  13.5 us
    pallas_call x5, Pallas kernels, fold(): pl.pallas_call(functools.partial(attend, count, tuple(shifts), begin, end...  4.91 us
    ppermute x6, waiting for transfers between devices, per_device(): up = [lax.ppermute(piece, 'ctx', ahead) for piece in up]  3.72 us
    ppermute x1, starting transfers between devices, per_device(): lax.ppermute(up[0], 'ctx', ahead)  1.96 us
    ppermute x1, waiting for transfers between devices, per_device(): lax.ppermute(down[1], 'ctx', back)  1.91 us
    ppermute x6, waiting for transfers between devices, per_device(): down = [lax.ppermute(piece, 'ctx', back) for piece in down]  1.47 us
    unnamed x5, local copies, waits for them, and re-layouts  1.04 us
  transfers between devices with their start and end apart: 14, of which 8 were waited for; matrix products, arithmetic and copies ran while one was open for 0% of the time, Pallas kernels for 11%

profile of v2, /device:TPU:0, one launch (start us, length us, event | category | flops | bytes accessed | tf_op | source)
XLA Modules:
  0.0 29.2 jit_solution(15006487894753144900)
XLA Ops:
  0.0 1.0 %copy.4 = bf16[16,8,2,512]{3,1,2,0:T(8,128)(2,1)S(1)} copy(bf16[16,8,2,512]{3,2,1,0:T(2,128)(2,1)} %bitcast.11) | data formatting | bytes 524288
  1.1 3.1 %collective-permute-start = (bf16[64,1024]{1,0:T(8,128)(2,1)S(1)}, bf16[64,1024]{1,0:T(8,128)(2,1)S(1)}, u32[]{:S(2)}, u32[]{:S(2)}) collective-permute-start(bf16[64,1024]{1,0:T(8,128)(2,1)S(1)} %get-tuple-element.54.refs_0_), channel_id=1, source_target_pairs={{0,2},{2,4},{4,6},{6,7},{7,5},{5,3},{3,1},{1,0},{8,10},{10,12},{12... | collective-permute-start | bytes 393224 | tf_op jit(solution)/shard_map/ppermute | solution.py:198
  4.2 0.0 collective-permute-start.4
  4.2 2.0 %collective-permute-start.2 = (bf16[64,1024]{1,0:T(8,128)(2,1)S(1)}, bf16[64,1024]{1,0:T(8,128)(2,1)S(1)}, u32[]{:S(2)}, u32[]{:S(2)}) collective-permute-start(bf16[64,1024]{1,0:T(8,128)(2,1)S(1)} %get-tuple-element.53.refs_1_), channel_id=1, source_target_pairs={{0,2},{2,4},{4,6},{6,7},{7,5},{5,3},{3,1},{1,0},{8,10},{10,12},{12... | collective-permute-start | bytes 393224 | tf_op jit(solution)/shard_map/ppermute | solution.py:198
  6.2 0.0 collective-permute-start.3
  6.2 0.8 %shard_map.37 = (f32[2,4,1,256]{3,2,1,0:T(1,128)S(1)}, f32[2,4,1,256]{3,2,1,0:T(1,128)S(1)}, f32[2,4,128,256]{3,2,1,0:T(8,128)S(1)}) custom-call(s32[1,16]{1,0:T(1,128)S(1)} %copy-done.1, bf16[128,2048]{1,0:T(8,128)(2,1)S(1)} %bitcast.5, bf16[64,1024]{1,0:T(8,128)(2,1)S(1)} %get-tuple-element.54.refs_0_, bf16[64,1024]{1,0:T(8,128)(2,1)S(1)} %get-tuple-element.53.refs_1_), custom_call_target="tpu_custom_call" | custom-call | flops 67108864 | bytes 1310720 | tf_op jit(solution)/shard_map/pallas_call | solution.py:166
  7.0 1.4 %collective-permute-done.refs_0_ = bf16[64,1024]{1,0:T(8,128)(2,1)S(1)} collective-permute-done((bf16[64,1024]{1,0:T(8,128)(2,1)S(1)}, bf16[64,1024]{1,0:T(8,128)(2,1)S(1)}, u32[]{:S(2)}, u32[]{:S(2)}) %collective-permute-start) | collective-permute-done | bytes 131104 | tf_op jit(solution)/shard_map/ppermute | solution.py:198
  8.4 2.1 %collective-permute-start.1 = (bf16[64,1024]{1,0:T(8,128)(2,1)S(1)}, bf16[64,1024]{1,0:T(8,128)(2,1)S(1)}, u32[]{:S(2)}, u32[]{:S(2)}) collective-permute-start(bf16[64,1024]{1,0:T(8,128)(2,1)S(1)} %collective-permute-done.refs_0_), channel_id=1, source_target_pairs={{0,2},{2,4},{4,6},{6,7},{7,5},{5,3},{3,1},{1,0},{8,10},{10,12},{12... | collective-permute-start | bytes 393224 | tf_op jit(solution)/shard_map/ppermute | solution.py:198
  10.5 0.0 collective-permute-done.4.refs_3_
  10.5 0.0 collective-permute-start.8
  10.6 0.7 %collective-permute-done.2.refs_1_ = bf16[64,1024]{1,0:T(8,128)(2,1)S(1)} collective-permute-done((bf16[64,1024]{1,0:T(8,128)(2,1)S(1)}, bf16[64,1024]{1,0:T(8,128)(2,1)S(1)}, u32[]{:S(2)}, u32[]{:S(2)}) %collective-permute-start.2) | collective-permute-done | bytes 131104 | tf_op jit(solution)/shard_map/ppermute | solution.py:198
  11.2 2.1 %collective-permute-start.6 = (bf16[64,1024]{1,0:T(8,128)(2,1)S(1)}, bf16[64,1024]{1,0:T(8,128)(2,1)S(1)}, u32[]{:S(2)}, u32[]{:S(2)}) collective-permute-start(bf16[64,1024]{1,0:T(8,128)(2,1)S(1)} %collective-permute-done.2.refs_1_), channel_id=1, source_target_pairs={{0,2},{2,4},{4,6},{6,7},{7,5},{5,3},{3,1},{1,0},{8,10},{10,12},{12... | collective-permute-start | bytes 393224 | tf_op jit(solution)/shard_map/ppermute | solution.py:198
  13.4 0.0 collective-permute-done.3.refs_2_
  13.4 0.0 collective-permute-start.7
  13.4 0.9 %shard_map.38 = (f32[2,4,1,256]{3,2,1,0:T(1,128)S(1)}, f32[2,4,1,256]{3,2,1,0:T(1,128)S(1)}, f32[2,4,128,256]{3,2,1,0:T(8,128)S(1)}) custom-call(s32[1,16]{1,0:T(1,128)S(1)} %copy-done.1, bf16[128,2048]{1,0:T(8,128)(2,1)S(1)} %bitcast.6, bf16[64,1024]{1,0:T(8,128)(2,1)S(1)} %collective-permute-done.refs_0_, ...), custom_call_target="tpu_custom_call" | custom-call | flops 134217728 | bytes 1572864 | tf_op jit(solution)/shard_map/pallas_call | solution.py:166
  14.2 0.3 %collective-permute-done.1.refs_0_ = bf16[64,1024]{1,0:T(8,128)(2,1)S(1)} collective-permute-done((bf16[64,1024]{1,0:T(8,128)(2,1)S(1)}, bf16[64,1024]{1,0:T(8,128)(2,1)S(1)}, u32[]{:S(2)}, u32[]{:S(2)}) %collective-permute-start.1) | collective-permute-done | bytes 131104 | tf_op jit(solution)/shard_map/ppermute | solution.py:198
  14.6 2.2 %collective-permute-start.5 = (bf16[64,1024]{1,0:T(8,128)(2,1)S(1)}, bf16[64,1024]{1,0:T(8,128)(2,1)S(1)}, u32[]{:S(2)}, u32[]{:S(2)}) collective-permute-start(bf16[64,1024]{1,0:T(8,128)(2,1)S(1)} %collective-permute-done.1.refs_0_), channel_id=1, source_target_pairs={{0,2},{2,4},{4,6},{6,7},{7,5},{5,3},{3,1},{1,0},{8,10},{10,12},{12... | collective-permute-start | bytes 393224 | tf_op jit(solution)/shard_map/ppermute | solution.py:198
  16.7 0.2 collective-permute-start.10
  16.9 0.8 %collective-permute-done.6.refs_1_ = bf16[64,1024]{1,0:T(8,128)(2,1)S(1)} collective-permute-done((bf16[64,1024]{1,0:T(8,128)(2,1)S(1)}, bf16[64,1024]{1,0:T(8,128)(2,1)S(1)}, u32[]{:S(2)}, u32[]{:S(2)}) %collective-permute-start.6) | collective-permute-done | bytes 131104 | tf_op jit(solution)/shard_map/ppermute | solution.py:198
  17.7 2.0 %collective-permute-start.12 = (bf16[64,1024]{1,0:T(8,128)(2,1)S(1)}, bf16[64,1024]{1,0:T(8,128)(2,1)S(1)}, u32[]{:S(2)}, u32[]{:S(2)}) collective-permute-start(bf16[64,1024]{1,0:T(8,128)(2,1)S(1)} %collective-permute-done.6.refs_1_), channel_id=1, source_target_pairs={{0,2},{2,4},{4,6},{6,7},{7,5},{5,3},{3,1},{1,0},{8,10},{10,12},{12... | collective-permute-start | bytes 393224 | tf_op jit(solution)/shard_map/ppermute | solution.py:198
  19.7 0.0 collective-permute-done.7.refs_2_
  19.7 0.1 collective-permute-start.13
  19.8 0.9 %shard_map.39 = (f32[2,4,1,256]{3,2,1,0:T(1,128)S(1)}, f32[2,4,1,256]{3,2,1,0:T(1,128)S(1)}, f32[2,4,128,256]{3,2,1,0:T(8,128)S(1)}) custom-call(s32[1,16]{1,0:T(1,128)S(1)} %copy-done.1, bf16[128,2048]{1,0:T(8,128)(2,1)S(1)} %bitcast.7, bf16[64,1024]{1,0:T(8,128)(2,1)S(1)} %collective-permute-done.1.refs_0_, ...), custom_call_target="tpu_custom_call" | custom-call | flops 134217728 | bytes 1572864 | tf_op jit(solution)/shard_map/pallas_call | solution.py:166
  20.7 2.0 %collective-permute-start.9 = (bf16[64,1024]{1,0:T(8,128)(2,1)S(1)}, bf16[64,1024]{1,0:T(8,128)(2,1)S(1)}, u32[]{:S(2)}, u32[]{:S(2)}) collective-permute-start(bf16[64,1024]{1,0:T(8,128)(2,1)S(1)} %collective-permute-done.5.refs_0_), channel_id=1, source_target_pairs={{0,2},{2,4},{4,6},{6,7},{7,5},{5,3},{3,1},{1,0},{8,10},{10,12},{12... | collective-permute-start | bytes 393224 | tf_op jit(solution)/shard_map/ppermute | solution.py:203
  22.6 0.0 collective-permute-done.10.refs_3_
  22.6 0.1 collective-permute-start.11
  22.8 0.5 %collective-permute-done.12.refs_1_ = bf16[64,1024]{1,0:T(8,128)(2,1)S(1)} collective-permute-done((bf16[64,1024]{1,0:T(8,128)(2,1)S(1)}, bf16[64,1024]{1,0:T(8,128)(2,1)S(1)}, u32[]{:S(2)}, u32[]{:S(2)}) %collective-permute-start.12) | collective-permute-done | bytes 131104 | tf_op jit(solution)/shard_map/ppermute | solution.py:198
  23.3 1.5 %collective-permute-done.13.refs_2_ = bf16[64,1024]{1,0:T(8,128)(2,1)S(1)} collective-permute-done((bf16[64,1024]{1,0:T(8,128)(2,1)S(1)}, bf16[64,1024]{1,0:T(8,128)(2,1)S(1)}, u32[]{:S(2)}, u32[]{:S(2)}) %collective-permute-start.13) | collective-permute-done | bytes 131104 | tf_op jit(solution)/shard_map/ppermute | solution.py:199
  24.7 0.9 %shard_map.40 = (f32[2,4,1,256]{3,2,1,0:T(1,128)S(1)}, f32[2,4,1,256]{3,2,1,0:T(1,128)S(1)}, f32[2,4,128,256]{3,2,1,0:T(8,128)S(1)}) custom-call(s32[1,16]{1,0:T(1,128)S(1)} %copy-done.1, bf16[128,2048]{1,0:T(8,128)(2,1)S(1)} %bitcast.8, bf16[64,1024]{1,0:T(8,128)(2,1)S(1)} %collective-permute-done.5.refs_0_, ...), custom_call_target="tpu_custom_call" | custom-call | flops 134217728 | bytes 1572864 | tf_op jit(solution)/shard_map/pallas_call | solution.py:166
  25.6 0.1 collective-permute-done.9.refs_0_
  25.7 1.9 %collective-permute-done.11.refs_1_ = bf16[64,1024]{1,0:T(8,128)(2,1)S(1)} collective-permute-done((bf16[64,1024]{1,0:T(8,128)(2,1)S(1)}, bf16[64,1024]{1,0:T(8,128)(2,1)S(1)}, u32[]{:S(2)}, u32[]{:S(2)}) %collective-permute-start.11) | collective-permute-done | bytes 131104 | tf_op jit(solution)/shard_map/ppermute | solution.py:203
  27.6 1.6 %shard_map.41 = bf16[128,2048]{1,0:T(8,128)(2,1)} custom-call(s32[1,16]{1,0:T(1,128)S(1)} %copy-done.1, bf16[128,2048]{1,0:T(8,128)(2,1)S(1)} %bitcast.9, bf16[64,1024]{1,0:T(8,128)(2,1)S(1)} %collective-permute-done.9.refs_0_, bf16[64,1024]{1,0:T(8,128)(2,1)S(1)} %collective-permute-done.11.refs_1_, f32[2,4,1,256]{3,2,1,0:T(1,128)S(1)} %get-tuple-element.50.refs_2_, ...), custom_call_target="tpu_custom_call" | custom-call | flops 67108864 | bytes 1310720 | tf_op jit(solution)/shard_map/pallas_call | solution.py:166
  (7 shorter events, 0.0 us)
Async XLA Ops:
  0.0 6.2 %copy-start = (bf16[1,128,2048]{2,1,0:T(8,128)(2,1)S(1)}, bf16[1,128,2048]{2,1,0:T(8,128)(2,1)}, u32[]{:S(2)}) copy-start(bf16[1,128,2048]{2,1,0:T(8,128)(2,1)} %param.3) | copy-start | bytes 1572868
  1.1 7.3 %collective-permute-start = (bf16[64,1024]{1,0:T(8,128)(2,1)S(1)}, bf16[64,1024]{1,0:T(8,128)(2,1)S(1)}, u32[]{:S(2)}, u32[]{:S(2)}) collective-permute-start(bf16[64,1024]{1,0:T(8,128)(2,1)S(1)} %get-tuple-element.54.refs_0_), channel_id=1, source_target_pairs={{0,2},{2,4},{4,6},{6,7},{7,5},{5,3},{3,1},{1,0},{8,10},{10,12},{12... | collective-permute-start | bytes 393224 | tf_op jit(solution)/shard_map/ppermute | solution.py:198
  4.1 2.1 %copy-start.1 = (s32[1,16]{1,0:T(1,128)S(1)}, s32[1,16]{1,0:T(1,128)}, u32[]{:S(2)}) copy-start(s32[1,16]{1,0:T(1,128)} %span_ref.9) | copy-start | bytes 196
  4.2 6.4 %collective-permute-start.4 = (bf16[64,1024]{1,0:T(8,128)(2,1)S(1)}, bf16[64,1024]{1,0:T(8,128)(2,1)S(1)}, u32[]{:S(2)}, u32[]{:S(2)}) collective-permute-start(bf16[64,1024]{1,0:T(8,128)(2,1)S(1)} %get-tuple-element.53.refs_1_), channel_id=1, source_target_pairs={{2,0},{4,2},{6,4},{7,6},{5,7},{3,5},{1,3},{0,1},{10,8},{12,10},{14... | collective-permute-start | bytes 393224 | tf_op jit(solution)/shard_map/ppermute | solution.py:199
  4.2 7.1 %collective-permute-start.2 = (bf16[64,1024]{1,0:T(8,128)(2,1)S(1)}, bf16[64,1024]{1,0:T(8,128)(2,1)S(1)}, u32[]{:S(2)}, u32[]{:S(2)}) collective-permute-start(bf16[64,1024]{1,0:T(8,128)(2,1)S(1)} %get-tuple-element.53.refs_1_), channel_id=1, source_target_pairs={{0,2},{2,4},{4,6},{6,7},{7,5},{5,3},{3,1},{1,0},{8,10},{10,12},{12... | collective-permute-start | bytes 393224 | tf_op jit(solution)/shard_map/ppermute | solution.py:198
  6.2 7.2 %collective-permute-start.3 = (bf16[64,1024]{1,0:T(8,128)(2,1)S(1)}, bf16[64,1024]{1,0:T(8,128)(2,1)S(1)}, u32[]{:S(2)}, u32[]{:S(2)}) collective-permute-start(bf16[64,1024]{1,0:T(8,128)(2,1)S(1)} %get-tuple-element.54.refs_0_), channel_id=1, source_target_pairs={{2,0},{4,2},{6,4},{7,6},{5,7},{3,5},{1,3},{0,1},{10,8},{12,10},{14... | collective-permute-start | bytes 393224 | tf_op jit(solution)/shard_map/ppermute | solution.py:199
  8.4 6.2 %collective-permute-start.1 = (bf16[64,1024]{1,0:T(8,128)(2,1)S(1)}, bf16[64,1024]{1,0:T(8,128)(2,1)S(1)}, u32[]{:S(2)}, u32[]{:S(2)}) collective-permute-start(bf16[64,1024]{1,0:T(8,128)(2,1)S(1)} %collective-permute-done.refs_0_), channel_id=1, source_target_pairs={{0,2},{2,4},{4,6},{6,7},{7,5},{5,3},{3,1},{1,0},{8,10},{10,12},{12... | collective-permute-start | bytes 393224 | tf_op jit(solution)/shard_map/ppermute | solution.py:198
  10.5 6.2 %collective-permute-start.8 = (bf16[64,1024]{1,0:T(8,128)(2,1)S(1)}, bf16[64,1024]{1,0:T(8,128)(2,1)S(1)}, u32[]{:S(2)}, u32[]{:S(2)}) collective-permute-start(bf16[64,1024]{1,0:T(8,128)(2,1)S(1)} %collective-permute-done.4.refs_3_), channel_id=1, source_target_pairs={{2,0},{4,2},{6,4},{7,6},{5,7},{3,5},{1,3},{0,1},{10,8},{12,10},{14... | collective-permute-start | bytes 393224 | tf_op jit(solution)/shard_map/ppermute | solution.py:199
  11.2 6.5 %collective-permute-start.6 = (bf16[64,1024]{1,0:T(8,128)(2,1)S(1)}, bf16[64,1024]{1,0:T(8,128)(2,1)S(1)}, u32[]{:S(2)}, u32[]{:S(2)}) collective-permute-start(bf16[64,1024]{1,0:T(8,128)(2,1)S(1)} %collective-permute-done.2.refs_1_), channel_id=1, source_target_pairs={{0,2},{2,4},{4,6},{6,7},{7,5},{5,3},{3,1},{1,0},{8,10},{10,12},{12... | collective-permute-start | bytes 393224 | tf_op jit(solution)/shard_map/ppermute | solution.py:198
  13.4 6.3 %collective-permute-start.7 = (bf16[64,1024]{1,0:T(8,128)(2,1)S(1)}, bf16[64,1024]{1,0:T(8,128)(2,1)S(1)}, u32[]{:S(2)}, u32[]{:S(2)}) collective-permute-start(bf16[64,1024]{1,0:T(8,128)(2,1)S(1)} %collective-permute-done.3.refs_2_), channel_id=1, source_target_pairs={{2,0},{4,2},{6,4},{7,6},{5,7},{3,5},{1,3},{0,1},{10,8},{12,10},{14... | collective-permute-start | bytes 393224 | tf_op jit(solution)/shard_map/ppermute | solution.py:199
  14.6 6.1 %collective-permute-start.5 = (bf16[64,1024]{1,0:T(8,128)(2,1)S(1)}, bf16[64,1024]{1,0:T(8,128)(2,1)S(1)}, u32[]{:S(2)}, u32[]{:S(2)}) collective-permute-start(bf16[64,1024]{1,0:T(8,128)(2,1)S(1)} %collective-permute-done.1.refs_0_), channel_id=1, source_target_pairs={{0,2},{2,4},{4,6},{6,7},{7,5},{5,3},{3,1},{1,0},{8,10},{10,12},{12... | collective-permute-start | bytes 393224 | tf_op jit(solution)/shard_map/ppermute | solution.py:198
  16.7 5.9 %collective-permute-start.10 = (bf16[64,1024]{1,0:T(8,128)(2,1)S(1)}, bf16[64,1024]{1,0:T(8,128)(2,1)S(1)}, u32[]{:S(2)}, u32[]{:S(2)}) collective-permute-start(bf16[64,1024]{1,0:T(8,128)(2,1)S(1)} %collective-permute-done.8.refs_3_), channel_id=1, source_target_pairs={{2,0},{4,2},{6,4},{7,6},{5,7},{3,5},{1,3},{0,1},{10,8},{12,10},{14... | collective-permute-start | bytes 393224 | tf_op jit(solution)/shard_map/ppermute | solution.py:199
  17.7 5.6 %collective-permute-start.12 = (bf16[64,1024]{1,0:T(8,128)(2,1)S(1)}, bf16[64,1024]{1,0:T(8,128)(2,1)S(1)}, u32[]{:S(2)}, u32[]{:S(2)}) collective-permute-start(bf16[64,1024]{1,0:T(8,128)(2,1)S(1)} %collective-permute-done.6.refs_1_), channel_id=1, source_target_pairs={{0,2},{2,4},{4,6},{6,7},{7,5},{5,3},{3,1},{1,0},{8,10},{10,12},{12... | collective-permute-start | bytes 393224 | tf_op jit(solution)/shard_map/ppermute | solution.py:198
  19.7 5.0 %collective-permute-start.13 = (bf16[64,1024]{1,0:T(8,128)(2,1)S(1)}, bf16[64,1024]{1,0:T(8,128)(2,1)S(1)}, u32[]{:S(2)}, u32[]{:S(2)}) collective-permute-start(bf16[64,1024]{1,0:T(8,128)(2,1)S(1)} %collective-permute-done.7.refs_2_), channel_id=1, source_target_pairs={{2,0},{4,2},{6,4},{7,6},{5,7},{3,5},{1,3},{0,1},{10,8},{12,10},{14... | collective-permute-start | bytes 393224 | tf_op jit(solution)/shard_map/ppermute | solution.py:199
  20.7 5.0 %collective-permute-start.9 = (bf16[64,1024]{1,0:T(8,128)(2,1)S(1)}, bf16[64,1024]{1,0:T(8,128)(2,1)S(1)}, u32[]{:S(2)}, u32[]{:S(2)}) collective-permute-start(bf16[64,1024]{1,0:T(8,128)(2,1)S(1)} %collective-permute-done.5.refs_0_), channel_id=1, source_target_pairs={{0,2},{2,4},{4,6},{6,7},{7,5},{5,3},{3,1},{1,0},{8,10},{10,12},{12... | collective-permute-start | bytes 393224 | tf_op jit(solution)/shard_map/ppermute | solution.py:203
  22.6 5.0 %collective-permute-start.11 = (bf16[64,1024]{1,0:T(8,128)(2,1)S(1)}, bf16[64,1024]{1,0:T(8,128)(2,1)S(1)}, u32[]{:S(2)}, u32[]{:S(2)}) collective-permute-start(bf16[64,1024]{1,0:T(8,128)(2,1)S(1)} %collective-permute-done.10.refs_3_), channel_id=1, source_target_pairs={{2,0},{4,2},{6,4},{7,6},{5,7},{3,5},{1,3},{0,1},{10,8},{12,10},{14... | collective-permute-start | bytes 393224 | tf_op jit(solution)/shard_map/ppermute | solution.py:203

commit v3 on v2

--- a/solution.py
+++ b/solution.py
@@ -35,6 +35,43 @@
 
 def value(piece, j):
     return piece[:, WIDTH + j * HEAD_DIM : WIDTH + (j + 1) * HEAD_DIM]
+
+
+def read_queries(q_ref, slot, rows, j):
+    start = slot * rows if isinstance(slot, int) else pl.multiple_of(slot * rows, rows)
+    return jnp.concatenate(
+        [
+            q_ref[pl.ds(start, rows), (j * GROUP + g) * HEAD_DIM : (j * GROUP + g + 1) * HEAD_DIM]
+            for g in range(GROUP)
+        ],
+        axis=0,
+    )
+
+
+def scores(k, q):
+    scale = math.log2(math.e) / math.sqrt(HEAD_DIM)
+    return lax.dot_general(k, q, NT, preferred_element_type=jnp.float32) * scale
+
+
+def weigh(v, p):
+    return lax.dot_general(v, p, TN, preferred_element_type=jnp.float32)
+
+
+def comes_before(count, shifts, span_ref):
+    place = ring_place(lax.axis_index("ctx"), count)
+    table = span_ref[...].astype(jnp.float32)
+    lane = lax.broadcasted_iota(jnp.int32, table.shape, 1)
+
+    def span_of(shift):
+        member = ring_member((place + shift + count) % count, count)
+        return jnp.sum(jnp.where(lane == 2 * member, table, 0.0))
+
+    own_span = span_of(0)
+    return [span_of(shift) < own_span for shift in shifts]
+
+
+def normalized(total, acc):
+    return (acc * (1.0 / total)).astype(jnp.bfloat16).T
 
 
 def attend(count, shifts, begin, end, span_ref, q_ref, *refs):
@@ -48,31 +85,9 @@
         top_out, total_out, acc_out = refs
     rows = chunks[0][0].shape[0]
     slot_rows = GROUP * rows
-    scale = math.log2(math.e) / math.sqrt(HEAD_DIM)
-    me = lax.axis_index("ctx")
-    place = ring_place(me, count)
-    table = span_ref[...].astype(jnp.float32)
-    lane = lax.broadcasted_iota(jnp.int32, table.shape, 1)
-
-    def span_of(member):
-        return jnp.sum(jnp.where(lane == 2 * member, table, 0.0))
-
 
     def queries(slot, j):
-        start = slot * rows if isinstance(slot, int) else pl.multiple_of(slot * rows, rows)
-        return jnp.concatenate(
-            [
-                q_ref[pl.ds(start, rows), (j * GROUP + g) * HEAD_DIM : (j * GROUP + g + 1) * HEAD_DIM]
-                for g in range(GROUP)
-            ],
-            axis=0,
-        )
-
-    def weigh(v, p):
-        return lax.dot_general(v, p, TN, preferred_element_type=jnp.float32)
-
-    def scores(k, q):
-        return lax.dot_general(k, q, NT, preferred_element_type=jnp.float32) * scale
+        return read_queries(q_ref, slot, rows, j)
 
     heads = range(KV_HEADS)
     result = {}
@@ -96,14 +111,12 @@
             p = jnp.exp2(s - new)
             result[1, j] = new, jnp.sum(p, axis=0, keepdims=True), weigh(v, p.astype(jnp.bfloat16))
     else:
-        own_span = span_of(me)
-        befores, slots, picked = [], [], []
-        for shift, (early, late) in zip(shifts, chunks):
-            other = ring_member((place + shift + count) % count, count)
-            befores.append(span_of(other) < own_span)
-            slots.append(jnp.where(befores[-1], 0, 1))
-            picked.append(jnp.where(befores[-1], early[...], late[...]))
         n = len(shifts)
+        befores = comes_before(count, shifts, span_ref)
+        slots = [jnp.where(before, 0, 1) for before in befores]
+        picked = [
+            jnp.where(before, early[...], late[...]) for before, (early, late) in zip(befores, chunks)
+        ]
         full, part = {}, {}
         for j in heads:
             k = jnp.concatenate([key(early, j) for early, _ in chunks], axis=0)
@@ -139,7 +152,7 @@
 
     for (slot, j), (new, added, update) in result.items():
         if end:
-            done = (update * (1.0 / added)).astype(jnp.bfloat16).T
+            done = normalized(added, update)
             for g in range(GROUP):
                 h = j * GROUP + g
                 out_ref[
@@ -149,6 +162,87 @@
             top_out[slot, j] = new
             total_out[slot, j] = added
             acc_out[slot, j] = update
+
+
+def fold_heads(old, piece, queries, counts):
+    heads = range(KV_HEADS)
+    s = [scores(key(piece, j), queries[j]) for j in heads]
+    most = [jnp.max(s[j], axis=0, keepdims=True) for j in heads]
+    if counts is not None:
+        most = [jnp.where(counts, most[j], -1e30) for j in heads]
+    new = [jnp.maximum(old[j][0], most[j]) for j in heads]
+    if counts is not None:
+        s = [jnp.where(counts, s[j], -1e30) for j in heads]
+    p = [jnp.exp2(s[j] - new[j]) for j in heads]
+    update = [weigh(value(piece, j), p[j].astype(jnp.bfloat16)) for j in heads]
+    shrink = [jnp.exp2(old[j][0] - new[j]) for j in heads]
+    total = [old[j][1] * shrink[j] + jnp.sum(p[j], axis=0, keepdims=True) for j in heads]
+    acc = [old[j][2] * shrink[j] + update[j] for j in heads]
+    return list(zip(new, total, acc))
+
+
+def finish(count, shift, slot, span_ref, q_ref, piece, *refs):
+    refs = list(refs)
+    top_in, total_in, acc_in = refs.pop(0), refs.pop(0), refs.pop(0)
+    if slot:
+        refs.pop(0)
+        out_ref, done, sems = refs
+    else:
+        out_ref, top_out, total_out, acc_out, done, sems = refs
+    rows = piece.shape[0]
+    (before,) = comes_before(count, [shift], span_ref)
+
+    def folded(i, counts):
+        old = [(top_in[i, j], total_in[i, j], acc_in[i, j]) for j in range(KV_HEADS)]
+        queries = [read_queries(q_ref, i, rows, j) for j in range(KV_HEADS)]
+        return fold_heads(old, piece, queries, counts)
+
+    states = folded(slot, jnp.logical_not(before) if slot else before)
+    copies = []
+    for j in range(KV_HEADS):
+        _, total, acc = states[j]
+        result = normalized(total, acc)
+        for g in range(GROUP):
+            h = j * GROUP + g
+            done[:, h * HEAD_DIM : (h + 1) * HEAD_DIM] = result[g * rows : (g + 1) * rows]
+        columns = slice(j * GROUP * HEAD_DIM, (j + 1) * GROUP * HEAD_DIM)
+        copies.append(
+            pltpu.make_async_copy(
+                done.at[:, columns], out_ref.at[slot * rows : (slot + 1) * rows, columns], sems.at[j]
+            )
+        )
+        copies[-1].start()
+    if not slot:
+        states = folded(1, None)
+        for j in range(KV_HEADS):
+            top_out[1, j], total_out[1, j], acc_out[1, j] = states[j]
+    for copy in copies:
+        copy.wait()
+
+
+def end(count, shift, slot, piece, state, out, span_ids, queries):
+    tok_rows, features = queries.shape
+    rows = tok_rows // 2
+    vmem, hbm = pl.BlockSpec(memory_space=pltpu.VMEM), pl.BlockSpec(memory_space=pltpu.HBM)
+    result = jax.ShapeDtypeStruct((tok_rows, features), queries.dtype)
+    like = [jax.ShapeDtypeStruct(part.shape, part.dtype) for part in state]
+    return pl.pallas_call(
+        functools.partial(finish, count, shift, slot),
+        out_shape=result if slot else [result, *like],
+        in_specs=[vmem] * 6 + [hbm] * slot,
+        out_specs=hbm if slot else [hbm] + [vmem] * 3,
+        scratch_shapes=[
+            pltpu.VMEM((rows, features), queries.dtype),
+            pltpu.SemaphoreType.DMA((KV_HEADS,)),
+        ],
+        input_output_aliases={6: 0} if slot else {},
+        compiler_params=pltpu.CompilerParams(vmem_limit_bytes=32 * 1024 * 1024),
+        cost_estimate=pl.CostEstimate(
+            flops=2 * tok_rows * features * rows,
+            bytes_accessed=4 * tok_rows * features,
+            transcendentals=rows * tok_rows * KV_HEADS * GROUP // 2,
+        ),
+    )(span_ids, queries, piece, *state, *([out] if slot else []))
 
 
 def fold(count, shifts, pieces, state, end, span_ids, queries):
@@ -192,7 +286,8 @@
     for step in range(1, last + 1):
         if step > 1:
             state = fold(count, *held, state, False, span_ids, queries[0])
-            up[0], *state = lax.optimization_barrier((up[0], *state))
+            if step == 2:
+                up[0], *state = lax.optimization_barrier((up[0], *state))
             held = shifts, pieces
         if 2 * step < count:
             up = [lax.ppermute(piece, "ctx", ahead) for piece in up]
@@ -204,7 +299,10 @@
     if last:
         state = fold(count, *held, state, False, span_ids, queries[0])
         held = shifts, pieces
-    return fold(count, *held, state, True, span_ids, queries[0])[None]
+    if count % 2:
+        return fold(count, *held, state, True, span_ids, queries[0])[None]
+    out, *state = end(count, shifts[0], 0, pieces[0], state, None, span_ids, queries[0])
+    return end(count, shifts[0], 1, pieces[1], state, out, span_ids, queries[0])[None]
 
 
 def solution(mesh):

time: 29.3 us -> 28.8 us (0.983)
  waiting for transfers between devices: 7.21 us -> 5.72 us
  Pallas kernels: 4.91 us -> 5.89 us
    pallas_call x0 -> x2, Pallas kernels: none -> 2.53 us  [end(): pl.pallas_call(functools.partial(finish, count, shift, slot), out_shape=r...]
    pallas_call x5 -> x4, Pallas kernels: 4.91 us -> 3.36 us  [fold(): pl.pallas_call(functools.partial(attend, count, tuple(shifts), begin, end...]
    ppermute x1, waiting for transfers between devices: 1.91 us -> 0.56 us  [per_device(): lax.ppermute(down[1], 'ctx', back)]
    ppermute x6, waiting for transfers between devices: 1.47 us -> 0.33 us  [per_device(): down = [lax.ppermute(piece, 'ctx', back) for piece in down]]
    ppermute x6, waiting for transfers between devices: 3.72 us -> 4.82 us  [per_device(): up = [lax.ppermute(piece, 'ctx', ahead) for piece in up]]
  transfers between devices with their start and end apart: 14 -> 14, of which waited for: 8 -> 7; matrix products, arithmetic and copies ran while one was open for 0% -> 0% of each run, Pallas kernels for 11% -> 16%
where the time goes in v3:
time: 28.8 us; the launch traced here: 28.7 us
  starting transfers between devices  15.9 us (55%)
  Pallas kernels  5.89 us (20%)
  waiting for transfers between devices  5.72 us (20%)
  local copies, waits for them, and re-layouts  1.06 us (4%)
    ppermute x6, starting transfers between devices, per_device(): up = [lax.ppermute(piece, 'ctx', ahead) for piece in up]  13.5 us
    ppermute x6, waiting for transfers between devices, per_device(): up = [lax.ppermute(piece, 'ctx', ahead) for piece in up]  4.82 us
    pallas_call x4, Pallas kernels, fold(): pl.pallas_call(functools.partial(attend, count, tuple(shifts), begin, end...  3.36 us
    pallas_call x2, Pallas kernels, end(): pl.pallas_call(functools.partial(finish, count, shift, slot), out_shape=r...  2.53 us
    ppermute x1, starting transfers between devices, per_device(): lax.ppermute(up[0], 'ctx', ahead)  1.98 us
    unnamed x5, local copies, waits for them, and re-layouts  1.04 us
  transfers between devices with their start and end apart: 14, of which 7 were waited for; matrix products, arithmetic and copies ran while one was open for 0% of the time, Pallas kernels for 16%

profile of v3, /device:TPU:0, one launch (start us, length us, event | category | flops | bytes accessed | tf_op | source)
XLA Modules:
  0.0 28.7 jit_solution(10877751616707700123)
XLA Ops:
  0.0 1.0 %copy.5 = bf16[16,8,2,512]{3,1,2,0:T(8,128)(2,1)S(1)} copy(bf16[16,8,2,512]{3,2,1,0:T(2,128)(2,1)} %bitcast.12) | data formatting | bytes 524288
  1.1 3.1 %collective-permute-start.4 = (bf16[64,1024]{1,0:T(8,128)(2,1)S(1)}, bf16[64,1024]{1,0:T(8,128)(2,1)S(1)}, u32[]{:S(2)}, u32[]{:S(2)}) collective-permute-start(bf16[64,1024]{1,0:T(8,128)(2,1)S(1)} %get-tuple-element.45.refs_0_), channel_id=1, source_target_pairs={{0,2},{2,4},{4,6},{6,7},{7,5},{5,3},{3,1},{1,0},{8,10},{10,12},{12... | collective-permute-start | bytes 393224 | tf_op jit(solution)/shard_map/ppermute | solution.py:293
  4.2 0.0 collective-permute-start
  4.2 2.0 %collective-permute-start.8 = (bf16[64,1024]{1,0:T(8,128)(2,1)S(1)}, bf16[64,1024]{1,0:T(8,128)(2,1)S(1)}, u32[]{:S(2)}, u32[]{:S(2)}) collective-permute-start(bf16[64,1024]{1,0:T(8,128)(2,1)S(1)} %get-tuple-element.46.refs_1_), channel_id=1, source_target_pairs={{0,2},{2,4},{4,6},{6,7},{7,5},{5,3},{3,1},{1,0},{8,10},{10,12},{12... | collective-permute-start | bytes 393224 | tf_op jit(solution)/shard_map/ppermute | solution.py:293
  6.2 0.0 collective-permute-start.11
  6.2 0.8 %shard_map.37 = (f32[2,4,1,256]{3,2,1,0:T(1,128)S(1)}, f32[2,4,1,256]{3,2,1,0:T(1,128)S(1)}, f32[2,4,128,256]{3,2,1,0:T(8,128)S(1)}) custom-call(s32[1,16]{1,0:T(1,128)S(1)} %copy-done.1, bf16[128,2048]{1,0:T(8,128)(2,1)S(1)} %bitcast.5, bf16[64,1024]{1,0:T(8,128)(2,1)S(1)} %get-tuple-element.45.refs_0_, bf16[64,1024]{1,0:T(8,128)(2,1)S(1)} %get-tuple-element.46.refs_1_), custom_call_target="tpu_custom_call" | custom-call | flops 67108864 | bytes 1310720 | tf_op jit(solution)/shard_map/pallas_call | solution.py:260
  7.0 1.4 %collective-permute-done.4.refs_0_ = bf16[64,1024]{1,0:T(8,128)(2,1)S(1)} collective-permute-done((bf16[64,1024]{1,0:T(8,128)(2,1)S(1)}, bf16[64,1024]{1,0:T(8,128)(2,1)S(1)}, u32[]{:S(2)}, u32[]{:S(2)}) %collective-permute-start.4) | collective-permute-done | bytes 131104 | tf_op jit(solution)/shard_map/ppermute | solution.py:293
  8.4 2.1 %collective-permute-start.5 = (bf16[64,1024]{1,0:T(8,128)(2,1)S(1)}, bf16[64,1024]{1,0:T(8,128)(2,1)S(1)}, u32[]{:S(2)}, u32[]{:S(2)}) collective-permute-start(bf16[64,1024]{1,0:T(8,128)(2,1)S(1)} %collective-permute-done.4.refs_0_), channel_id=1, source_target_pairs={{0,2},{2,4},{4,6},{6,7},{7,5},{5,3},{3,1},{1,0},{8,10},{10,12},{12... | collective-permute-start | bytes 393224 | tf_op jit(solution)/shard_map/ppermute | solution.py:293
  10.5 0.0 collective-permute-done.refs_3_
  10.5 0.0 collective-permute-start.1
  10.6 0.7 %collective-permute-done.8.refs_1_ = bf16[64,1024]{1,0:T(8,128)(2,1)S(1)} collective-permute-done((bf16[64,1024]{1,0:T(8,128)(2,1)S(1)}, bf16[64,1024]{1,0:T(8,128)(2,1)S(1)}, u32[]{:S(2)}, u32[]{:S(2)}) %collective-permute-start.8) | collective-permute-done | bytes 131104 | tf_op jit(solution)/shard_map/ppermute | solution.py:293
  11.2 2.1 %collective-permute-start.9 = (bf16[64,1024]{1,0:T(8,128)(2,1)S(1)}, bf16[64,1024]{1,0:T(8,128)(2,1)S(1)}, u32[]{:S(2)}, u32[]{:S(2)}) collective-permute-start(bf16[64,1024]{1,0:T(8,128)(2,1)S(1)} %collective-permute-done.8.refs_1_), channel_id=1, source_target_pairs={{0,2},{2,4},{4,6},{6,7},{7,5},{5,3},{3,1},{1,0},{8,10},{10,12},{12... | collective-permute-start | bytes 393224 | tf_op jit(solution)/shard_map/ppermute | solution.py:293
  13.4 0.0 collective-permute-done.11.refs_2_
  13.4 1.2 %collective-permute-done.5.refs_0_ = bf16[64,1024]{1,0:T(8,128)(2,1)S(1)} collective-permute-done((bf16[64,1024]{1,0:T(8,128)(2,1)S(1)}, bf16[64,1024]{1,0:T(8,128)(2,1)S(1)}, u32[]{:S(2)}, u32[]{:S(2)}) %collective-permute-start.5) | collective-permute-done | bytes 131104 | tf_op jit(solution)/shard_map/ppermute | solution.py:293
  14.6 2.2 %collective-permute-start.6 = (bf16[64,1024]{1,0:T(8,128)(2,1)S(1)}, bf16[64,1024]{1,0:T(8,128)(2,1)S(1)}, u32[]{:S(2)}, u32[]{:S(2)}) collective-permute-start(bf16[64,1024]{1,0:T(8,128)(2,1)S(1)} %collective-permute-done.5.refs_0_), channel_id=1, source_target_pairs={{0,2},{2,4},{4,6},{6,7},{7,5},{5,3},{3,1},{1,0},{8,10},{10,12},{12... | collective-permute-start | bytes 393224 | tf_op jit(solution)/shard_map/ppermute | solution.py:293
  16.7 0.0 collective-permute-done.1.refs_3_
  16.7 0.2 collective-permute-start.2
  16.9 0.8 %collective-permute-done.9.refs_1_ = bf16[64,1024]{1,0:T(8,128)(2,1)S(1)} collective-permute-done((bf16[64,1024]{1,0:T(8,128)(2,1)S(1)}, bf16[64,1024]{1,0:T(8,128)(2,1)S(1)}, u32[]{:S(2)}, u32[]{:S(2)}) %collective-permute-start.9) | collective-permute-done | bytes 131104 | tf_op jit(solution)/shard_map/ppermute | solution.py:293
  17.7 2.0 %collective-permute-start.10 = (bf16[64,1024]{1,0:T(8,128)(2,1)S(1)}, bf16[64,1024]{1,0:T(8,128)(2,1)S(1)}, u32[]{:S(2)}, u32[]{:S(2)}) collective-permute-start(bf16[64,1024]{1,0:T(8,128)(2,1)S(1)} %collective-permute-done.9.refs_1_), channel_id=1, source_target_pairs={{0,2},{2,4},{4,6},{6,7},{7,5},{5,3},{3,1},{1,0},{8,10},{10,12},{12... | collective-permute-start | bytes 393224 | tf_op jit(solution)/shard_map/ppermute | solution.py:293
  19.7 0.0 collective-permute-done.12.refs_2_
  19.7 0.1 collective-permute-start.13
  19.8 0.7 %collective-permute-done.6.refs_0_ = bf16[64,1024]{1,0:T(8,128)(2,1)S(1)} collective-permute-done((bf16[64,1024]{1,0:T(8,128)(2,1)S(1)}, bf16[64,1024]{1,0:T(8,128)(2,1)S(1)}, u32[]{:S(2)}, u32[]{:S(2)}) %collective-permute-start.6) | collective-permute-done | bytes 131104 | tf_op jit(solution)/shard_map/ppermute | solution.py:293
  20.5 2.0 %collective-permute-start.7 = (bf16[64,1024]{1,0:T(8,128)(2,1)S(1)}, bf16[64,1024]{1,0:T(8,128)(2,1)S(1)}, u32[]{:S(2)}, u32[]{:S(2)}) collective-permute-start(bf16[64,1024]{1,0:T(8,128)(2,1)S(1)} %collective-permute-done.6.refs_0_), channel_id=1, source_target_pairs={{0,2},{2,4},{4,6},{6,7},{7,5},{5,3},{3,1},{1,0},{8,10},{10,12},{12... | collective-permute-start | bytes 393224 | tf_op jit(solution)/shard_map/ppermute | solution.py:298
  22.5 0.1 collective-permute-start.3
  22.6 0.9 %shard_map.38 = (f32[2,4,1,256]{3,2,1,0:T(1,128)S(1)}, f32[2,4,1,256]{3,2,1,0:T(1,128)S(1)}, f32[2,4,128,256]{3,2,1,0:T(8,128)S(1)}) custom-call(s32[1,16]{1,0:T(1,128)S(1)} %copy-done.1, bf16[128,2048]{1,0:T(8,128)(2,1)S(1)} %bitcast.6, bf16[64,1024]{1,0:T(8,128)(2,1)S(1)} %collective-permute-done.4.refs_0_, ...), custom_call_target="tpu_custom_call" | custom-call | flops 134217728 | bytes 1572864 | tf_op jit(solution)/shard_map/pallas_call | solution.py:260
  23.5 0.9 %shard_map.39 = (f32[2,4,1,256]{3,2,1,0:T(1,128)S(1)}, f32[2,4,1,256]{3,2,1,0:T(1,128)S(1)}, f32[2,4,128,256]{3,2,1,0:T(8,128)S(1)}) custom-call(s32[1,16]{1,0:T(1,128)S(1)} %copy-done.1, bf16[128,2048]{1,0:T(8,128)(2,1)S(1)} %bitcast.7, bf16[64,1024]{1,0:T(8,128)(2,1)S(1)} %collective-permute-done.5.refs_0_, ...), custom_call_target="tpu_custom_call" | custom-call | flops 134217728 | bytes 1572864 | tf_op jit(solution)/shard_map/pallas_call | solution.py:260
  24.4 0.0 collective-permute-done.10.refs_1_
  24.4 0.3 %collective-permute-done.13.refs_2_ = bf16[64,1024]{1,0:T(8,128)(2,1)S(1)} collective-permute-done((bf16[64,1024]{1,0:T(8,128)(2,1)S(1)}, bf16[64,1024]{1,0:T(8,128)(2,1)S(1)}, u32[]{:S(2)}, u32[]{:S(2)}) %collective-permute-start.13) | collective-permute-done | bytes 131104 | tf_op jit(solution)/shard_map/ppermute | solution.py:294
  24.7 0.9 %shard_map.40 = (f32[2,4,1,256]{3,2,1,0:T(1,128)S(1)}, f32[2,4,1,256]{3,2,1,0:T(1,128)S(1)}, f32[2,4,128,256]{3,2,1,0:T(8,128)S(1)}) custom-call(s32[1,16]{1,0:T(1,128)S(1)} %copy-done.1, bf16[128,2048]{1,0:T(8,128)(2,1)S(1)} %bitcast.8, bf16[64,1024]{1,0:T(8,128)(2,1)S(1)} %collective-permute-done.6.refs_0_, ...), custom_call_target="tpu_custom_call" | custom-call | flops 134217728 | bytes 1572864 | tf_op jit(solution)/shard_map/pallas_call | solution.py:260
  25.6 1.3 %shard_map.41 = (bf16[128,2048]{1,0:T(8,128)(2,1)}, f32[2,4,1,256]{3,2,1,0:T(1,128)S(1)}, f32[2,4,1,256]{3,2,1,0:T(1,128)S(1)}, f32[2,4,128,256]{3,2,1,0:T(8,128)S(1)}) custom-call(s32[1,16]{1,0:T(1,128)S(1)} %copy-done.1, bf16[128,2048]{1,0:T(8,128)(2,1)S(1)} %bitcast.9, bf16[64,1024]{1,0:T(8,128)(2,1)S(1)} %collective-permute-done.7.piece, ...), custom_call_target="tpu_custom_call" | custom-call | flops 33554432 | bytes 1048576 | tf_op jit(solution)/shard_map/pallas_call | solution.py:229
  26.9 0.6 %collective-permute-done.3.piece = bf16[64,1024]{1,0:T(8,128)(2,1)S(1)} collective-permute-done((bf16[64,1024]{1,0:T(8,128)(2,1)S(1)}, bf16[64,1024]{1,0:T(8,128)(2,1)S(1)}, u32[]{:S(2)}, u32[]{:S(2)}) %collective-permute-start.3) | collective-permute-done | bytes 131104 | tf_op jit(solution)/shard_map/ppermute | solution.py:298
  27.5 1.2 %shard_map.42 = bf16[128,2048]{1,0:T(8,128)(2,1)} custom-call(s32[1,16]{1,0:T(1,128)S(1)} %copy-done.1, bf16[128,2048]{1,0:T(8,128)(2,1)S(1)} %bitcast.10, bf16[64,1024]{1,0:T(8,128)(2,1)S(1)} %collective-permute-done.3.piece, f32[2,4,1,256]{3,2,1,0:T(1,128)S(1)} %get-tuple-element.41.refs_0_, ...), custom_call_target="tpu_custom_call", output_to_operand_aliasing={{}: (6, {})} | custom-call | flops 33554432 | bytes 1048576 | tf_op jit(solution)/shard_map/pallas_call | solution.py:229
  (8 shorter events, 0.0 us)
Async XLA Ops:
  0.0 6.2 %copy-start = (bf16[1,128,2048]{2,1,0:T(8,128)(2,1)S(1)}, bf16[1,128,2048]{2,1,0:T(8,128)(2,1)}, u32[]{:S(2)}) copy-start(bf16[1,128,2048]{2,1,0:T(8,128)(2,1)} %param.3) | copy-start | bytes 1572868
  1.1 7.3 %collective-permute-start.4 = (bf16[64,1024]{1,0:T(8,128)(2,1)S(1)}, bf16[64,1024]{1,0:T(8,128)(2,1)S(1)}, u32[]{:S(2)}, u32[]{:S(2)}) collective-permute-start(bf16[64,1024]{1,0:T(8,128)(2,1)S(1)} %get-tuple-element.45.refs_0_), channel_id=1, source_target_pairs={{0,2},{2,4},{4,6},{6,7},{7,5},{5,3},{3,1},{1,0},{8,10},{10,12},{12... | collective-permute-start | bytes 393224 | tf_op jit(solution)/shard_map/ppermute | solution.py:293
  4.1 2.1 %copy-start.1 = (s32[1,16]{1,0:T(1,128)S(1)}, s32[1,16]{1,0:T(1,128)}, u32[]{:S(2)}) copy-start(s32[1,16]{1,0:T(1,128)} %span_ref.11) | copy-start | bytes 196
  4.2 6.4 %collective-permute-start = (bf16[64,1024]{1,0:T(8,128)(2,1)S(1)}, bf16[64,1024]{1,0:T(8,128)(2,1)S(1)}, u32[]{:S(2)}, u32[]{:S(2)}) collective-permute-start(bf16[64,1024]{1,0:T(8,128)(2,1)S(1)} %get-tuple-element.46.refs_1_), channel_id=1, source_target_pairs={{2,0},{4,2},{6,4},{7,6},{5,7},{3,5},{1,3},{0,1},{10,8},{12,10},{14... | collective-permute-start | bytes 393224 | tf_op jit(solution)/shard_map/ppermute | solution.py:294
  4.2 7.1 %collective-permute-start.8 = (bf16[64,1024]{1,0:T(8,128)(2,1)S(1)}, bf16[64,1024]{1,0:T(8,128)(2,1)S(1)}, u32[]{:S(2)}, u32[]{:S(2)}) collective-permute-start(bf16[64,1024]{1,0:T(8,128)(2,1)S(1)} %get-tuple-element.46.refs_1_), channel_id=1, source_target_pairs={{0,2},{2,4},{4,6},{6,7},{7,5},{5,3},{3,1},{1,0},{8,10},{10,12},{12... | collective-permute-start | bytes 393224 | tf_op jit(solution)/shard_map/ppermute | solution.py:293
  6.2 7.2 %collective-permute-start.11 = (bf16[64,1024]{1,0:T(8,128)(2,1)S(1)}, bf16[64,1024]{1,0:T(8,128)(2,1)S(1)}, u32[]{:S(2)}, u32[]{:S(2)}) collective-permute-start(bf16[64,1024]{1,0:T(8,128)(2,1)S(1)} %get-tuple-element.45.refs_0_), channel_id=1, source_target_pairs={{2,0},{4,2},{6,4},{7,6},{5,7},{3,5},{1,3},{0,1},{10,8},{12,10},{14... | collective-permute-start | bytes 393224 | tf_op jit(solution)/shard_map/ppermute | solution.py:294
  8.4 6.2 %collective-permute-start.5 = (bf16[64,1024]{1,0:T(8,128)(2,1)S(1)}, bf16[64,1024]{1,0:T(8,128)(2,1)S(1)}, u32[]{:S(2)}, u32[]{:S(2)}) collective-permute-start(bf16[64,1024]{1,0:T(8,128)(2,1)S(1)} %collective-permute-done.4.refs_0_), channel_id=1, source_target_pairs={{0,2},{2,4},{4,6},{6,7},{7,5},{5,3},{3,1},{1,0},{8,10},{10,12},{12... | collective-permute-start | bytes 393224 | tf_op jit(solution)/shard_map/ppermute | solution.py:293
  10.5 6.2 %collective-permute-start.1 = (bf16[64,1024]{1,0:T(8,128)(2,1)S(1)}, bf16[64,1024]{1,0:T(8,128)(2,1)S(1)}, u32[]{:S(2)}, u32[]{:S(2)}) collective-permute-start(bf16[64,1024]{1,0:T(8,128)(2,1)S(1)} %collective-permute-done.refs_3_), channel_id=1, source_target_pairs={{2,0},{4,2},{6,4},{7,6},{5,7},{3,5},{1,3},{0,1},{10,8},{12,10},{14... | collective-permute-start | bytes 393224 | tf_op jit(solution)/shard_map/ppermute | solution.py:294
  11.2 6.5 %collective-permute-start.9 = (bf16[64,1024]{1,0:T(8,128)(2,1)S(1)}, bf16[64,1024]{1,0:T(8,128)(2,1)S(1)}, u32[]{:S(2)}, u32[]{:S(2)}) collective-permute-start(bf16[64,1024]{1,0:T(8,128)(2,1)S(1)} %collective-permute-done.8.refs_1_), channel_id=1, source_target_pairs={{0,2},{2,4},{4,6},{6,7},{7,5},{5,3},{3,1},{1,0},{8,10},{10,12},{12... | collective-permute-start | bytes 393224 | tf_op jit(solution)/shard_map/ppermute | solution.py:293
  13.4 6.3 %collective-permute-start.12 = (bf16[64,1024]{1,0:T(8,128)(2,1)S(1)}, bf16[64,1024]{1,0:T(8,128)(2,1)S(1)}, u32[]{:S(2)}, u32[]{:S(2)}) collective-permute-start(bf16[64,1024]{1,0:T(8,128)(2,1)S(1)} %collective-permute-done.11.refs_2_), channel_id=1, source_target_pairs={{2,0},{4,2},{6,4},{7,6},{5,7},{3,5},{1,3},{0,1},{10,8},{12,10},{14... | collective-permute-start | bytes 393224 | tf_op jit(solution)/shard_map/ppermute | solution.py:294
  14.6 6.0 %collective-permute-start.6 = (bf16[64,1024]{1,0:T(8,128)(2,1)S(1)}, bf16[64,1024]{1,0:T(8,128)(2,1)S(1)}, u32[]{:S(2)}, u32[]{:S(2)}) collective-permute-start(bf16[64,1024]{1,0:T(8,128)(2,1)S(1)} %collective-permute-done.5.refs_0_), channel_id=1, source_target_pairs={{0,2},{2,4},{4,6},{6,7},{7,5},{5,3},{3,1},{1,0},{8,10},{10,12},{12... | collective-permute-start | bytes 393224 | tf_op jit(solution)/shard_map/ppermute | solution.py:293
  16.7 5.8 %collective-permute-start.2 = (bf16[64,1024]{1,0:T(8,128)(2,1)S(1)}, bf16[64,1024]{1,0:T(8,128)(2,1)S(1)}, u32[]{:S(2)}, u32[]{:S(2)}) collective-permute-start(bf16[64,1024]{1,0:T(8,128)(2,1)S(1)} %collective-permute-done.1.refs_3_), channel_id=1, source_target_pairs={{2,0},{4,2},{6,4},{7,6},{5,7},{3,5},{1,3},{0,1},{10,8},{12,10},{14... | collective-permute-start | bytes 393224 | tf_op jit(solution)/shard_map/ppermute | solution.py:294
  17.7 6.7 %collective-permute-start.10 = (bf16[64,1024]{1,0:T(8,128)(2,1)S(1)}, bf16[64,1024]{1,0:T(8,128)(2,1)S(1)}, u32[]{:S(2)}, u32[]{:S(2)}) collective-permute-start(bf16[64,1024]{1,0:T(8,128)(2,1)S(1)} %collective-permute-done.9.refs_1_), channel_id=1, source_target_pairs={{0,2},{2,4},{4,6},{6,7},{7,5},{5,3},{3,1},{1,0},{8,10},{10,12},{12... | collective-permute-start | bytes 393224 | tf_op jit(solution)/shard_map/ppermute | solution.py:293
  19.7 5.0 %collective-permute-start.13 = (bf16[64,1024]{1,0:T(8,128)(2,1)S(1)}, bf16[64,1024]{1,0:T(8,128)(2,1)S(1)}, u32[]{:S(2)}, u32[]{:S(2)}) collective-permute-start(bf16[64,1024]{1,0:T(8,128)(2,1)S(1)} %collective-permute-done.12.refs_2_), channel_id=1, source_target_pairs={{2,0},{4,2},{6,4},{7,6},{5,7},{3,5},{1,3},{0,1},{10,8},{12,10},{14... | collective-permute-start | bytes 393224 | tf_op jit(solution)/shard_map/ppermute | solution.py:294
  20.5 5.0 %collective-permute-start.7 = (bf16[64,1024]{1,0:T(8,128)(2,1)S(1)}, bf16[64,1024]{1,0:T(8,128)(2,1)S(1)}, u32[]{:S(2)}, u32[]{:S(2)}) collective-permute-start(bf16[64,1024]{1,0:T(8,128)(2,1)S(1)} %collective-permute-done.6.refs_0_), channel_id=1, source_target_pairs={{0,2},{2,4},{4,6},{6,7},{7,5},{5,3},{3,1},{1,0},{8,10},{10,12},{12... | collective-permute-start | bytes 393224 | tf_op jit(solution)/shard_map/ppermute | solution.py:298
  22.5 5.0 %collective-permute-start.3 = (bf16[64,1024]{1,0:T(8,128)(2,1)S(1)}, bf16[64,1024]{1,0:T(8,128)(2,1)S(1)}, u32[]{:S(2)}, u32[]{:S(2)}) collective-permute-start(bf16[64,1024]{1,0:T(8,128)(2,1)S(1)} %collective-permute-done.2.refs_3_), channel_id=1, source_target_pairs={{2,0},{4,2},{6,4},{7,6},{5,7},{3,5},{1,3},{0,1},{10,8},{12,10},{14... | collective-permute-start | bytes 393224 | tf_op jit(solution)/shard_map/ppermute | solution.py:298
